TPU v7x, 32 devices: a whole 2x2x4 slice. The times are simulated.
32 devices in a mesh: chan: 16 (over z, x, core), tm: 2 (over y).
Axes of the slice: x: 2, y: 2, z: 4, core: 2. Of those that a mesh axis runs over, the one named last changes fastest.
Arguments:
- raw_strain: bfloat16 [2048, 16384], P('chan', 'tm'), may hold values from -6 to 6
- fir_taps: bfloat16 [64], replicated, may hold values from -0.75 to 0.75
- sources: int32 [2, 8], replicated, may hold values from 0 to 2047, as said below
Outputs:
- correlation: float32 [2, 8, 257, 2048], P(None, 'tm', None, 'chan')
Inputs may be any that keep to these rules, and one draw needn't show every extreme that they name: `sources`: the 16 entries are distinct channel indices; the first and the last channel are always among them.
All inputs are finite; a program needn't handle non-finite values.
Results may differ from a plain program's by a relative error of at most 0.0037.
Values may be sent and summed in bfloat16 or wider, within the bound.
A program may use at most 64 MiB of HBM per device.

v0:
```python
import functools
import math

import jax
import jax.numpy as jnp
from jax import lax
from jax.experimental import pallas as pl
from jax.experimental.pallas import tpu as pltpu
from jax.sharding import PartitionSpec as P

TAPS = 64
DECIM = 4
HALF_WIN = 32
LAGS = 257
HALF_LAG = 128
STEPS = 2
W = 128
SLAB = 8
PIECES = 4
LEFT = 256
RIGHT = 128
MESH = pl.DeviceIdType.MESH


def nt(a, b):
    return lax.dot_general(
        a, b, (((1,), (1,)), ((), ())), preferred_element_type=jnp.float32
    )


def aligned(x):
    return pl.multiple_of(x, W)


def kernel(
    C, T, scale,
    raw_ref, taps_hbm, src_hbm, out_ref,
    taps_ref, src_ref, praw_ref, rep_ref, x_ref, dec_ref, hi_ref, lo_ref, white_ref, send1, recv1, recv2, gref, acc_ref,
    small_sem, load_sem, halo_send, halo_recv, s1_sem, r1_sem, s2_sem, r2_sem, own_sem, bulk_send, bulk_recv,
):
    c = lax.axis_index("chan")
    t = lax.axis_index("tm")
    N = C * T
    rows, raw_len = raw_ref.shape
    dec_len = raw_len // DECIM
    nb = dec_len // W
    per_dev = (T * nb) // C
    half = nb // per_dev
    step_len = src_hbm.shape[1] // T
    ns = STEPS * step_len
    me = c * T + t

    barrier = pltpu.get_barrier_semaphore()

    def greet(d, _):
        other = lax.rem(me + d, N)
        pl.semaphore_signal(
            barrier, inc=1, device_id=(other // T, lax.rem(other, T)), device_id_type=MESH
        )
        return 0

    lax.fori_loop(1, N, greet, 0)

    small = [
        pltpu.make_async_copy(taps_hbm, taps_ref, small_sem.at[0]),
        pltpu.make_async_copy(src_hbm, src_ref, small_sem.at[1]),
    ]
    for copy in small:
        copy.start()
    seg = raw_len // PIECES
    loads = []
    for i in range(PIECES):
        load = pltpu.make_async_copy(
            raw_ref.at[:, pl.ds(i * seg, seg)],
            x_ref.at[:, pl.ds(LEFT + i * seg, seg)],
            load_sem.at[i],
        )
        load.start()
        loads.append(load)

    for copy in small:
        copy.wait()

    taps = jnp.broadcast_to(taps_ref[...], (16, TAPS))
    place = lax.broadcasted_iota(jnp.int32, (TAPS, W), 1) == lax.rem(
        W - lax.broadcasted_iota(jnp.int32, (TAPS, W), 0), W
    )
    base = jnp.dot(
        taps, place.astype(jnp.float32).astype(jnp.bfloat16), preferred_element_type=jnp.float32
    )
    rolled = pltpu.roll(
        jnp.broadcast_to(base[0:1, :], (W, W)), 0, 1, stride=DECIM, stride_axis=0
    )
    row_id = lax.broadcasted_iota(jnp.int32, (W, W), 0)
    lane_id = lax.broadcasted_iota(jnp.int32, (W, W), 1)
    fts = []
    for jc in range(DECIM + 1):
        k = DECIM * row_id + W - W * jc - lane_id
        fts.append(jnp.where((k >= 0) & (k < W), rolled, 0.0).astype(jnp.bfloat16))
    ft = jnp.concatenate(fts, axis=1)

    pr = lax.broadcasted_iota(jnp.int32, (T * SLAB, rows), 0)
    pc = lax.broadcasted_iota(jnp.int32, (T * SLAB, rows), 1)
    picks = jnp.zeros((T * SLAB, rows), jnp.float32)
    for g in range(T):
        for step in range(STEPS):
            for p in range(step_len):
                local = src_ref[step, g * step_len + p] - c * rows
                hit = (pr == g * SLAB + step * step_len + p) & (pc == local)
                picks = jnp.where(hit, 1.0, picks)
    picks = picks.astype(jnp.bfloat16)

    pl.semaphore_wait(barrier, N - 1)

    to_right = pltpu.make_async_remote_copy(
        src_ref=raw_ref.at[:, pl.ds(raw_len - LEFT, LEFT)],
        dst_ref=x_ref.at[:, pl.ds(0, LEFT)],
        send_sem=halo_send.at[0], recv_sem=halo_recv.at[0],
        device_id=(c, lax.rem(t + 1, T)), device_id_type=MESH,
    )
    to_left = pltpu.make_async_remote_copy(
        src_ref=raw_ref.at[:, pl.ds(0, RIGHT)],
        dst_ref=x_ref.at[:, pl.ds(LEFT + raw_len, RIGHT)],
        send_sem=halo_send.at[1], recv_sem=halo_recv.at[1],
        device_id=(c, lax.rem(t + T - 1, T)), device_id_type=MESH,
    )

    @pl.when(t < T - 1)
    def _():
        to_right.start()

    @pl.when(t > 0)
    def _():
        to_left.start()

    @pl.when(t == 0)
    def _():
        x_ref[:, 0:LEFT] = jnp.zeros((rows, LEFT), jnp.bfloat16)

    @pl.when(t == T - 1)
    def _():
        x_ref[:, LEFT + raw_len:] = jnp.zeros((rows, RIGHT), jnp.bfloat16)

    total = T * dec_len
    white_ref[:, 0:W] = jnp.zeros((rows, W), jnp.bfloat16)
    white_ref[:, W + total:] = jnp.zeros((rows, W), jnp.bfloat16)

    def put_mag(b, d):
        mag = jnp.abs(d)
        hi = mag.astype(jnp.bfloat16)
        hi_ref[:, (b + 1) * W:(b + 2) * W] = hi
        lo_ref[:, (b + 1) * W:(b + 2) * W] = (mag - hi.astype(jnp.float32)).astype(jnp.bfloat16)

    def chunk(b):
        begin = LEFT - W + b * DECIM * W
        d = nt(x_ref[:, begin:begin + (DECIM + 1) * W], ft)
        dec_ref[:, b * W:(b + 1) * W] = d
        put_mag(b, d)

    def pick_raw(x):
        return jnp.dot(picks, x, preferred_element_type=jnp.float32).astype(jnp.bfloat16)

    lead = (DECIM + 1) * W
    many = T * SLAB
    praw_ref[:, 0:lead - LEFT] = jnp.zeros((many, lead - LEFT), jnp.bfloat16)
    praw_ref[:, lead + raw_len + RIGHT:] = jnp.zeros((many, DECIM * W - RIGHT), jnp.bfloat16)
    for i in range(PIECES):
        loads[i].wait()
        praw_ref[:, lead + i * seg:lead + (i + 1) * seg] = pick_raw(
            x_ref[:, LEFT + i * seg:LEFT + (i + 1) * seg]
        )
    for b in range(1, nb):
        chunk(b)

    @pl.when(t > 0)
    def _():
        to_right.wait_recv()

    @pl.when(t < T - 1)
    def _():
        to_left.wait_recv()

    praw_ref[:, lead - LEFT:lead] = pick_raw(x_ref[:, 0:LEFT])
    praw_ref[:, lead + raw_len:lead + raw_len + RIGHT] = pick_raw(x_ref[:, LEFT + raw_len:])
    picked = nt(
        jnp.concatenate(
            [praw_ref[:, b * DECIM * W:b * DECIM * W + lead] for b in range(nb + 2)], axis=0
        ),
        ft,
    )
    size = (nb + 2) * many
    pr = lax.broadcasted_iota(jnp.int32, (size, W), 0)
    pc = lax.broadcasted_iota(jnp.int32, (size, W), 1)
    inside = ((pr >= many) | ((t > 0) & (pc >= W - HALF_WIN))) & (
        (pr < size - many) | ((t < T - 1) & (pc < HALF_WIN))
    )
    mag = jnp.where(inside, jnp.abs(picked), 0.0)
    hi = mag.astype(jnp.bfloat16)
    lo = (mag - hi.astype(jnp.float32)).astype(jnp.bfloat16)
    wide = jnp.concatenate(
        [m[k * many:k * many + nb * many] for m in (hi, lo) for k in range(3)], axis=1
    )
    span = lax.broadcasted_iota(jnp.int32, (W, 3 * W), 1) - W - lax.broadcasted_iota(
        jnp.int32, (W, 3 * W), 0
    )
    band = jnp.where((span >= -HALF_WIN) & (span <= HALF_WIN), 1.0, 0.0).astype(jnp.bfloat16)
    level = nt(wide, jnp.concatenate([band, band], axis=1)) / (2 * HALF_WIN + 1) + 1e-05
    picked = picked[many:many + nb * many] / level
    for g in range(T):
        for i in range(half):
            send1[g * half + i] = jnp.concatenate(
                [
                    picked[q * many + g * SLAB:q * many + (g + 1) * SLAB]
                    for q in (2 * i, 2 * i + 1)
                ],
                axis=0,
            ).astype(jnp.bfloat16)

    def first(k, go):
        g, i = k // half, k % half
        dest = t * half + i
        self_hit = (dest == c) & (g == t)
        remote = pltpu.make_async_remote_copy(
            src_ref=send1.at[k], dst_ref=recv1.at[c],
            send_sem=s1_sem.at[k], recv_sem=r1_sem,
            device_id=(dest, g), device_id_type=MESH,
        )

        @pl.when(jnp.logical_not(self_hit))
        def _():
            if go:
                remote.start()
            else:
                remote.wait_send()

        if go:
            @pl.when(self_hit)
            def _():
                pltpu.make_async_copy(send1.at[k], recv1.at[c], r1_sem).start()

    def each(count, body):
        if count <= 16:
            for i in range(count):
                body(i)
            return

        def step(i, _):
            body(i)
            return 0

        lax.fori_loop(0, count, step, 0)

    each(T * half, lambda k: first(k, True))

    chunk(0)
    before = nt(x_ref[:, 0:LEFT], ft[:, 3 * W:5 * W])
    keep = (t > 0) & (lax.broadcasted_iota(jnp.int32, (rows, W), 1) >= W - HALF_WIN)
    put_mag(-1, jnp.where(keep, before, 0.0))
    after = nt(x_ref[:, LEFT + raw_len - W:LEFT + raw_len + RIGHT], ft[:, 0:2 * W])
    keep = (t < T - 1) & (lax.broadcasted_iota(jnp.int32, (rows, W), 1) < HALF_WIN)
    put_mag(nb, jnp.where(keep, after, 0.0))

    span = lax.broadcasted_iota(jnp.int32, (2 * W, 4 * W), 1) - W - lax.broadcasted_iota(
        jnp.int32, (2 * W, 4 * W), 0
    )
    band = jnp.where((span >= -HALF_WIN) & (span <= HALF_WIN), 1.0, 0.0).astype(jnp.bfloat16)
    mine = W + t * dec_len

    piece = dec_len // PIECES

    def bulk(d, i):
        cols = pl.ds(aligned(mine + i * piece), piece)
        return pltpu.make_async_remote_copy(
            src_ref=white_ref.at[:, cols], dst_ref=white_ref.at[:, cols],
            send_sem=bulk_send.at[d - 1, i], recv_sem=bulk_recv.at[d - 1, i],
            device_id=(c, lax.rem(t + d, T)), device_id_type=MESH,
        )

    for p in range(nb // 2):
        cols = slice(2 * p * W, (2 * p + 4) * W)
        sums = nt(hi_ref[:, cols], band) + nt(lo_ref[:, cols], band)
        level = sums / (2 * HALF_WIN + 1) + 1e-05
        w = (dec_ref[:, 2 * p * W:2 * (p + 1) * W] / level).astype(jnp.bfloat16)
        white_ref[:, pl.ds(aligned(mine + 2 * p * W), 2 * W)] = w
        if (2 * p + 2) * W % piece == 0:
            for d in range(1, T):
                bulk(d, (2 * p + 2) * W // piece - 1).start()

    pltpu.make_async_copy(recv1, recv1, r1_sem).wait()
    summed = recv1[0].astype(jnp.float32)
    for j in range(1, C):
        summed = summed + recv1[j].astype(jnp.float32)
    send1[T * half] = summed.astype(jnp.bfloat16)

    def second(d):
        return pltpu.make_async_remote_copy(
            src_ref=send1.at[T * half], dst_ref=recv2.at[c],
            send_sem=s2_sem.at[d], recv_sem=r2_sem,
            device_id=(lax.rem(c + d + 1, C), t), device_id_type=MESH,
        )

    each(C - 1, lambda d: second(d).start())
    pltpu.make_async_copy(send1.at[T * half], recv2.at[c], r2_sem).start()
    pltpu.make_async_copy(recv2, recv2, r2_sem).wait()

    group = 16 // step_len
    main = ns * W
    gathered = jnp.concatenate([recv2[j] for j in range(C)], axis=1)
    spread_row = lax.broadcasted_iota(jnp.int32, (2 * STEPS * 16, 16), 0)
    spread_col = lax.broadcasted_iota(jnp.int32, (2 * STEPS * 16, 16), 1)
    wanted = (spread_row // (STEPS * 16)) * SLAB + (spread_row // 16 % STEPS) * step_len + (
        spread_row % step_len
    )
    spread = jnp.where(spread_col == wanted, 1.0, 0.0).astype(jnp.bfloat16)
    rep_ref[...] = jnp.dot(spread, gathered, preferred_element_type=jnp.float32).astype(
        jnp.bfloat16
    )
    slabs = gathered.astype(jnp.float32)
    gref[main:main + 16, 0:W] = jnp.zeros((16, W), jnp.bfloat16)
    for q in range(2 * C):
        slab = slabs[q % 2 * SLAB:(q % 2 + 1) * SLAB, q // 2 * W:(q // 2 + 1) * W]
        gref[main:main + 16, (q + 1) * W:(q + 2) * W] = jnp.concatenate(
            [slab, slab], axis=0
        ).astype(jnp.bfloat16)
    low = (lax.broadcasted_iota(jnp.int32, (16, W), 0) // step_len)
    low_lane = (lax.broadcasted_iota(jnp.int32, (16, W), 1) - low).astype(jnp.int16)
    low = low.astype(jnp.int16)
    tiles = W // group
    for step in range(STEPS):
        first_row = step * step_len * W

        def tile(a, now, prev, column):
            gref[first_row + a * 16:first_row + (a + 1) * 16, pl.ds(column, W)] = jnp.where(
                low_lane >= a * group, now, prev
            )

        def build(j, prev):
            for h in range(2):
                top = (h * STEPS + step) * 16
                x = rep_ref[top:top + 16, pl.ds(aligned(j * W), W)]
                start = x
                for k in range(1, group):
                    start = jnp.where(low == k, pltpu.roll(x, k, 1), start)
                out = []
                for a in range(tiles):
                    now = pltpu.roll(start, a * group, 1) if a else start
                    tile(a, now, prev[a], aligned((2 * j + h) * W))
                    out.append(now)
                prev = tuple(out)
            return prev

        last = lax.fori_loop(0, C, build, (jnp.zeros((16, W), jnp.bfloat16),) * tiles)
        for a in range(tiles):
            tile(a, jnp.zeros((16, W), jnp.bfloat16), last[a], total)

    def products(a, count):
        both = jnp.concatenate(
            [
                white_ref[:, pl.ds(aligned(a * W), count * W)],
                white_ref[:, pl.ds(aligned(a * W + W), count * W)],
            ],
            axis=0,
        )
        return nt(gref[:, pl.ds(aligned(a * W), count * W)], both)

    acc_ref[...] = products(t * nb + 1, nb - 1)
    step_chunks = nb // PIECES
    for d in range(1, T):
        b = lax.rem(t + T - d, T)
        for i in range(PIECES):
            bulk_in = pltpu.make_async_copy(
                white_ref.at[:, pl.ds(aligned(W + b * dec_len + i * piece), piece)],
                white_ref.at[:, pl.ds(aligned(W + b * dec_len + i * piece), piece)],
                bulk_recv.at[d - 1, i],
            )
            bulk_in.wait()
            skip = 1 if i == 0 else 0
            acc_ref[...] += products(b * nb + i * step_chunks + skip, step_chunks - skip)
    seams = [q * nb * W for q in range(T + 1)]
    both = jnp.concatenate(
        [
            jnp.concatenate([white_ref[:, q:q + W] for q in seams], axis=1),
            jnp.concatenate([white_ref[:, q + W:q + 2 * W] for q in seams], axis=1),
        ],
        axis=0,
    )
    acc_ref[...] += nt(jnp.concatenate([gref[:, q:q + W] for q in seams], axis=1), both)

    span = step_len * W
    for step in range(STEPS):
        at, to = step * span, step * step_len * LAGS
        out_ref[to:to + span, :] = acc_ref[at:at + span, 0:W] * scale
        out_ref[to + span:to + 2 * span, :] = acc_ref[at:at + span, W:2 * W] * scale
        extra = main + step * step_len
        out_ref[to + 2 * span:to + 2 * span + step_len, :] = (
            acc_ref[extra:extra + step_len, W:2 * W] * scale
        )

    @pl.when(t < T - 1)
    def _():
        to_right.wait_send()

    @pl.when(t > 0)
    def _():
        to_left.wait_send()

    each(T * half, lambda k: first(k, False))
    each(C - 1, lambda d: second(d).wait_send())
    for d in range(1, T):
        for i in range(PIECES):
            bulk(d, i).wait_send()


def per_device(C, T, raw_strain, fir_taps, sources):
    rows, raw_len = raw_strain.shape
    dec_len = raw_len // DECIM
    nb = dec_len // W
    half = nb * C // (T * nb)
    step_len = sources.shape[1] // T
    ns = STEPS * step_len
    total = T * dec_len
    bf, f32 = jnp.bfloat16, jnp.float32
    flat = pl.pallas_call(
        functools.partial(kernel, C, T, 1.0 / math.sqrt(total)),
        out_shape=pltpu.VMEM((STEPS * LAGS * step_len, rows), f32),
        in_specs=[
            pl.BlockSpec(memory_space=pltpu.HBM),
            pl.BlockSpec(memory_space=pltpu.HBM),
            pl.BlockSpec(memory_space=pltpu.HBM),
        ],
        out_specs=pl.BlockSpec(memory_space=pltpu.VMEM),
        scratch_shapes=[
            pltpu.VMEM((1, TAPS), bf),
            pltpu.SMEM(sources.shape, jnp.int32),
            pltpu.VMEM((T * SLAB, raw_len + (2 * DECIM + 1) * W), bf),
            pltpu.VMEM((2 * STEPS * 16, C * W), bf),
            pltpu.VMEM((rows, LEFT + raw_len + RIGHT), bf),
            pltpu.VMEM((rows, dec_len), f32),
            pltpu.VMEM((rows, dec_len + 2 * W), bf),
            pltpu.VMEM((rows, dec_len + 2 * W), bf),
            pltpu.VMEM((rows, total + 2 * W), bf),
            pltpu.VMEM((T * half + 1, 16, W), bf),
            pltpu.VMEM((C, 16, W), bf),
            pltpu.VMEM((C, 16, W), bf),
            pltpu.VMEM((ns * W + 16, total + W), bf),
            pltpu.VMEM((ns * W + 16, 2 * W), f32),
            pltpu.SemaphoreType.DMA((2,)),
            pltpu.SemaphoreType.DMA((PIECES,)),
            pltpu.SemaphoreType.DMA((2,)),
            pltpu.SemaphoreType.DMA((2,)),
            pltpu.SemaphoreType.DMA((T * half,)),
            pltpu.SemaphoreType.DMA,
            pltpu.SemaphoreType.DMA((C,)),
            pltpu.SemaphoreType.DMA,
            pltpu.SemaphoreType.DMA,
            pltpu.SemaphoreType.DMA((T, PIECES)),
            pltpu.SemaphoreType.DMA((T, PIECES)),
        ],
        compiler_params=pltpu.CompilerParams(
            collective_id=0, has_side_effects=True, vmem_limit_bytes=62 * 1024 * 1024
        ),
    )(raw_strain, fir_taps.reshape(1, TAPS), sources)
    return jnp.swapaxes(flat.reshape(STEPS, LAGS, step_len, rows), 1, 2)


def solution(mesh):
    C, T = mesh.shape["chan"], mesh.shape["tm"]
    return jax.shard_map(
        functools.partial(per_device, C, T),
        mesh=mesh,
        in_specs=(P("chan", "tm"), P(), P()),
        out_specs=P(None, "tm", None, "chan"),
        check_vma=False,
    )
```

profile of v0, /device:TPU:0, one launch (start us, length us, event | category | flops | bytes accessed | tf_op | source)
XLA Modules:
  0.0 33.4 jit_solution(12982286405405561307)
XLA Ops:
  0.0 32.5 %shard_map.37 = f32[2056,128]{1,0:T(8,128)S(1)} custom-call(bf16[128,8192]{1,0:T(8,128)(2,1)} %raw_ref.1, bf16[1,64]{1,0:T(2,128)(2,1)} %bitcast.5, s32[2,8]{1,0:T(2,128)} %src_hbm.1), custom_call_target="tpu_custom_call" | custom-call | tf_op jit(solution)/shard_map/pallas_call | solution.py:423
  32.5 1.0 %copy.5 = f32[2,4,257,128]{3,1,2,0:T(4,128)} copy(f32[2,4,257,128]{3,1,2,0:T(4,128)S(1)} %bitcast.4) | data formatting | bytes 2105344
where the time goes:
time: 33.6 us; the launch traced here: 33.4 us
  Pallas kernels  32.5 us (97%)
  local copies, waits for them, and re-layouts  0.97 us (3%)
    pallas_call x1, Pallas kernels, per_device(): pl.pallas_call(functools.partial(kernel, C, T, 1.0 / math.sqrt(total)), o...  32.5 us
    unnamed x1, local copies, waits for them, and re-layouts  0.97 us

commit v1 on v0

v1 whole, which is shorter than its diff:
```python
import functools
import math

import jax
import jax.numpy as jnp
from jax import lax
from jax.experimental import pallas as pl
from jax.experimental.pallas import tpu as pltpu
from jax.sharding import PartitionSpec as P

TAPS = 64
DECIM = 4
HALF_WIN = 32
LAGS = 257
HALF_LAG = 128
STEPS = 2
W = 128
SLAB = 8
EARLY = 3
BLOCK = 1024
LEFT = 256
RIGHT = 128
MESH = pl.DeviceIdType.MESH


def nt(a, b):
    return lax.dot_general(
        a, b, (((1,), (1,)), ((), ())), preferred_element_type=jnp.float32
    )


def aligned(x):
    return pl.multiple_of(x, W)


def kernel(
    C, T, scale,
    raw_ref, taps_hbm, src_hbm, out_ref,
    taps_ref, src_ref, x_ref, dec_ref, hi_ref, lo_ref, white_ref, send1, recv1, recv2, rep_ref, shifted, acc_ref,
    small_sem, load_sem, halo_send, halo_recv, s1_sem, r1_sem, s2_sem, r2_sem, bulk_send, bulk_recv,
):
    c = lax.axis_index("chan")
    t = lax.axis_index("tm")
    N = C * T
    rows, raw_len = raw_ref.shape
    dec_len = raw_len // DECIM
    nb = dec_len // W
    half = nb // ((T * nb) // C)
    step_len = src_hbm.shape[1] // T
    ns = STEPS * step_len
    me = c * T + t
    total = T * dec_len
    mine = t * dec_len

    barrier = pltpu.get_barrier_semaphore()

    def greet(d, _):
        other = lax.rem(me + d, N)
        pl.semaphore_signal(
            barrier, inc=1, device_id=(other // T, lax.rem(other, T)), device_id_type=MESH
        )
        return 0

    lax.fori_loop(1, N, greet, 0)

    small = [
        pltpu.make_async_copy(taps_hbm, taps_ref, small_sem.at[0]),
        pltpu.make_async_copy(src_hbm, src_ref, small_sem.at[1]),
    ]
    for copy in small:
        copy.start()
    seg = raw_len // half
    loads = []
    for i in range(half):
        load = pltpu.make_async_copy(
            raw_ref.at[:, pl.ds(i * seg, seg)],
            x_ref.at[:, pl.ds(LEFT + i * seg, seg)],
            load_sem.at[i],
        )
        load.start()
        loads.append(load)

    span = lax.broadcasted_iota(jnp.int32, (2 * W, 4 * W), 1) - W - lax.broadcasted_iota(
        jnp.int32, (2 * W, 4 * W), 0
    )
    band = jnp.where((span >= -HALF_WIN) & (span <= HALF_WIN), 1.0, 0.0).astype(jnp.bfloat16)

    for copy in small:
        copy.wait()

    taps = jnp.broadcast_to(taps_ref[...], (16, TAPS))
    place = lax.broadcasted_iota(jnp.int32, (TAPS, W), 1) == lax.rem(
        W - lax.broadcasted_iota(jnp.int32, (TAPS, W), 0), W
    )
    base = jnp.dot(
        taps, place.astype(jnp.float32).astype(jnp.bfloat16), preferred_element_type=jnp.float32
    )
    rolled = pltpu.roll(
        jnp.broadcast_to(base[0:1, :], (W, W)), 0, 1, stride=DECIM, stride_axis=0
    )
    row_id = lax.broadcasted_iota(jnp.int32, (W, W), 0)
    lane_id = lax.broadcasted_iota(jnp.int32, (W, W), 1)
    fts = []
    for jc in range(DECIM + 1):
        k = DECIM * row_id + W - W * jc - lane_id
        fts.append(jnp.where((k >= 0) & (k < W), rolled, 0.0).astype(jnp.bfloat16))
    ft = jnp.concatenate(fts, axis=1)

    pr = lax.broadcasted_iota(jnp.int32, (T * SLAB, rows), 0)
    pc = lax.broadcasted_iota(jnp.int32, (T * SLAB, rows), 1)
    picks = jnp.zeros((T * SLAB, rows), jnp.float32)
    for g in range(T):
        for step in range(STEPS):
            for p in range(step_len):
                local = src_ref[step, g * step_len + p] - c * rows
                hit = (pr == g * SLAB + step * step_len + p) & (pc == local)
                picks = jnp.where(hit, 1.0, picks)
    picks = picks.astype(jnp.bfloat16)

    to_right = pltpu.make_async_remote_copy(
        src_ref=raw_ref.at[:, pl.ds(raw_len - LEFT, LEFT)],
        dst_ref=x_ref.at[:, pl.ds(0, LEFT)],
        send_sem=halo_send.at[0], recv_sem=halo_recv.at[0],
        device_id=(c, lax.rem(t + 1, T)), device_id_type=MESH,
    )
    to_left = pltpu.make_async_remote_copy(
        src_ref=raw_ref.at[:, pl.ds(0, RIGHT)],
        dst_ref=x_ref.at[:, pl.ds(LEFT + raw_len, RIGHT)],
        send_sem=halo_send.at[1], recv_sem=halo_recv.at[1],
        device_id=(c, lax.rem(t + T - 1, T)), device_id_type=MESH,
    )

    def put_mag(b, d):
        mag = jnp.abs(d)
        hi = mag.astype(jnp.bfloat16)
        hi_ref[:, (b + 1) * W:(b + 2) * W] = hi
        lo_ref[:, (b + 1) * W:(b + 2) * W] = (mag - hi.astype(jnp.float32)).astype(jnp.bfloat16)

    def chunk(b):
        begin = LEFT - W + b * DECIM * W
        d = nt(x_ref[:, begin:begin + (DECIM + 1) * W], ft)
        dec_ref[:, b * W:(b + 1) * W] = d
        put_mag(b, d)

    def first(g, i):
        k = g * half + i
        dest = t * half + i
        self_hit = (dest == c) & (g == t)
        remote = pltpu.make_async_remote_copy(
            src_ref=send1.at[k], dst_ref=recv1.at[c],
            send_sem=s1_sem.at[k], recv_sem=r1_sem,
            device_id=(dest, g), device_id_type=MESH,
        )
        return self_hit, remote

    def start_first(g, i):
        self_hit, remote = first(g, i)

        @pl.when(jnp.logical_not(self_hit))
        def _():
            remote.start()

        @pl.when(self_hit)
        def _():
            pltpu.make_async_copy(send1.at[g * half + i], recv1.at[c], r1_sem).start()

    def end_first(g, i):
        self_hit, remote = first(g, i)

        @pl.when(jnp.logical_not(self_hit))
        def _():
            remote.wait_send()

    def bulk(d, i):
        cols = pl.ds(aligned(mine + i * 2 * W), 2 * W)
        return pltpu.make_async_remote_copy(
            src_ref=white_ref.at[:, cols], dst_ref=white_ref.at[:, cols],
            send_sem=bulk_send.at[d - 1, i], recv_sem=bulk_recv.at[d - 1, i],
            device_id=(c, lax.rem(t + d, T)), device_id_type=MESH,
        )

    def pair(p):
        cols = slice(2 * p * W, (2 * p + 4) * W)
        sums = nt(hi_ref[:, cols], band) + nt(lo_ref[:, cols], band)
        level = sums / (2 * HALF_WIN + 1) + 1e-05
        w = (dec_ref[:, 2 * p * W:2 * (p + 1) * W] / level).astype(jnp.bfloat16)
        white_ref[:, pl.ds(aligned(mine + 2 * p * W), 2 * W)] = w
        picked = jnp.dot(picks, w, preferred_element_type=jnp.float32)
        for g in range(T):
            send1[g * half + p] = jnp.concatenate(
                [picked[g * SLAB:(g + 1) * SLAB, h * W:(h + 1) * W] for h in range(2)], axis=0
            ).astype(jnp.bfloat16)

    def all_bulk(i):
        for d in range(1, T):
            bulk(d, i).start()

    order = list(range(1, half - 1)) + [0, half - 1]
    done = {0}
    here = 0
    for at, p in enumerate(order):
        if p == 0:
            @pl.when(t > 0)
            def _():
                to_right.wait_recv()

            @pl.when(t < T - 1)
            def _():
                to_left.wait_recv()

            chunk(0)
            before = nt(x_ref[:, 0:LEFT], ft[:, 3 * W:5 * W])
            keep = (t > 0) & (lax.broadcasted_iota(jnp.int32, (rows, W), 1) >= W - HALF_WIN)
            put_mag(-1, jnp.where(keep, before, 0.0))
            after = nt(x_ref[:, LEFT + raw_len - W:LEFT + raw_len + RIGHT], ft[:, 0:2 * W])
            keep = (t < T - 1) & (lax.broadcasted_iota(jnp.int32, (rows, W), 1) < HALF_WIN)
            put_mag(nb, jnp.where(keep, after, 0.0))
        for b in range(2 * p - 1, min(2 * p + 3, nb)):
            if b >= 0 and b not in done:
                while here <= b // 2:
                    loads[here].wait()
                    here += 1
                chunk(b)
                done.add(b)
        pair(p)
        if at == 0:
            pl.semaphore_wait(barrier, N - 1)

            @pl.when(t < T - 1)
            def _():
                to_right.start()

            @pl.when(t > 0)
            def _():
                to_left.start()

            @pl.when(t == 0)
            def _():
                x_ref[:, 0:LEFT] = jnp.zeros((rows, LEFT), jnp.bfloat16)

            @pl.when(t == T - 1)
            def _():
                x_ref[:, LEFT + raw_len:] = jnp.zeros((rows, RIGHT), jnp.bfloat16)

        for g in range(T):
            start_first(g, p)
        if at < EARLY:
            all_bulk(p)

    shifted[0:W, :] = jnp.zeros((W, W), jnp.bfloat16)

    def each(count, body):
        if count <= 16:
            for i in range(count):
                body(i)
            return

        def step(i, _):
            body(i)
            return 0

        lax.fori_loop(0, count, step, 0)

    pltpu.make_async_copy(recv1, recv1, r1_sem).wait()
    summed = recv1[0].astype(jnp.float32)
    for j in range(1, C):
        summed = summed + recv1[j].astype(jnp.float32)
    send1[T * half] = summed.astype(jnp.bfloat16)

    def second(d):
        return pltpu.make_async_remote_copy(
            src_ref=send1.at[T * half], dst_ref=recv2.at[c],
            send_sem=s2_sem.at[d], recv_sem=r2_sem,
            device_id=(lax.rem(c + d + 1, C), t), device_id_type=MESH,
        )

    each(C - 1, lambda d: second(d).start())
    pltpu.make_async_copy(send1.at[T * half], recv2.at[c], r2_sem).start()
    for i in order[EARLY:]:
        all_bulk(i)
    pltpu.make_async_copy(recv2, recv2, r2_sem).wait()

    lags = W // ns
    tall = lags * step_len
    tiles = tall // SLAB
    group = SLAB // step_len
    gathered = jnp.concatenate([recv2[j] for j in range(C)], axis=1)
    spread_row = lax.broadcasted_iota(jnp.int32, (2 * STEPS * SLAB, 2 * SLAB), 0)
    spread_col = lax.broadcasted_iota(jnp.int32, (2 * STEPS * SLAB, 2 * SLAB), 1)
    wanted = (spread_row // (STEPS * SLAB)) * SLAB + (spread_row // SLAB % STEPS) * step_len + (
        spread_row % step_len
    )
    spread = jnp.where(spread_col == wanted, 1.0, 0.0).astype(jnp.bfloat16)
    rep_ref[...] = jnp.dot(spread, gathered, preferred_element_type=jnp.float32)
    low = lax.broadcasted_iota(jnp.int32, (SLAB, W), 0) // step_len
    low_lane = lax.broadcasted_iota(jnp.int32, (SLAB, W), 1) - low
    zero = jnp.zeros((SLAB, W), jnp.float32)

    def build(j, prev):
        for h in range(2):
            now = []
            for step in range(STEPS):
                top = (h * STEPS + step) * SLAB
                x = rep_ref[top:top + SLAB, pl.ds(aligned(j * W), W)]
                start = x
                for k in range(1, group):
                    start = jnp.where(low == k, pltpu.roll(x, k, 1), start)
                for v in range(tiles):
                    now.append(pltpu.roll(start, v * group, 1) if v else start)
            put_shifted(aligned((2 * j + h + 1) * W), now, prev)
            prev = tuple(now)
        return prev

    def put_shifted(at, now, prev):
        z = jnp.concatenate(
            [
                jnp.where(low_lane >= (v % tiles) * group, now[v], prev[v])
                for v in range(STEPS * tiles)
            ],
            axis=0,
        )
        shifted[pl.ds(at, W), :] = z.T.astype(jnp.bfloat16)

    last = lax.fori_loop(0, C, build, (zero,) * (STEPS * tiles))
    put_shifted(W + total, (zero,) * (STEPS * tiles), last)

    groups = 2 * HALF_LAG // lags + 1

    def products(n, count, fresh=False):
        w = white_ref[:, pl.ds(aligned(n), count)]
        for k in range(0, groups, 2):
            b = jnp.concatenate(
                [
                    shifted[pl.ds(pl.multiple_of(n + 2 * HALF_LAG - lags * m, 16), count), :]
                    for m in range(k, min(k + 2, groups))
                ],
                axis=1,
            )
            out = jnp.dot(w, b, preferred_element_type=jnp.float32)
            cols = slice(k * W, k * W + b.shape[1])
            if fresh:
                acc_ref[:, cols] = out
            else:
                acc_ref[:, cols] += out

    block = min(BLOCK, dec_len)
    for q in range(dec_len // block):
        products(mine + q * block, block, q == 0)

    def arrive(d, i):
        at = lax.rem(t + T - d, T) * dec_len + i * 2 * W
        cols = pl.ds(aligned(at), 2 * W)
        pltpu.make_async_copy(
            white_ref.at[:, cols], white_ref.at[:, cols], bulk_recv.at[d - 1, i]
        ).wait()
        products(at, 2 * W)

    def arrivals(d, _):
        for i in order:
            arrive(d, i)
        return 0

    if T == 2:
        arrivals(1, 0)
    else:
        lax.fori_loop(1, T, arrivals, 0)

    for k in range(groups):
        block = acc_ref[:, k * W:(k + 1) * W].T * scale
        for step in range(STEPS):
            to = (step * LAGS + k * lags) * step_len
            size = tall if k < groups - 1 else step_len
            out_ref[to:to + size, :] = block[step * tall:step * tall + size, :]

    @pl.when(t < T - 1)
    def _():
        to_right.wait_send()

    @pl.when(t > 0)
    def _():
        to_left.wait_send()

    for g in range(T):
        each(half, lambda i: end_first(g, i))
    each(C - 1, lambda d: second(d).wait_send())
    for d in range(1, T):
        for i in range(half):
            bulk(d, i).wait_send()


def per_device(C, T, raw_strain, fir_taps, sources):
    rows, raw_len = raw_strain.shape
    dec_len = raw_len // DECIM
    nb = dec_len // W
    half = nb * C // (T * nb)
    step_len = sources.shape[1] // T
    ns = STEPS * step_len
    total = T * dec_len
    groups = 2 * HALF_LAG // (W // ns) + 1
    bf, f32 = jnp.bfloat16, jnp.float32
    flat = pl.pallas_call(
        functools.partial(kernel, C, T, 1.0 / math.sqrt(total)),
        out_shape=pltpu.VMEM((STEPS * LAGS * step_len, rows), f32),
        in_specs=[
            pl.BlockSpec(memory_space=pltpu.HBM),
            pl.BlockSpec(memory_space=pltpu.HBM),
            pl.BlockSpec(memory_space=pltpu.HBM),
        ],
        out_specs=pl.BlockSpec(memory_space=pltpu.VMEM),
        scratch_shapes=[
            pltpu.VMEM((1, TAPS), bf),
            pltpu.SMEM(sources.shape, jnp.int32),
            pltpu.VMEM((rows, LEFT + raw_len + RIGHT), bf),
            pltpu.VMEM((rows, dec_len), f32),
            pltpu.VMEM((rows, dec_len + 2 * W), bf),
            pltpu.VMEM((rows, dec_len + 2 * W), bf),
            pltpu.VMEM((rows, total), bf),
            pltpu.VMEM((T * half + 1, 16, W), bf),
            pltpu.VMEM((C, 16, W), bf),
            pltpu.VMEM((C, 16, W), bf),
            pltpu.VMEM((2 * STEPS * SLAB, C * W), f32),
            pltpu.VMEM((total + 2 * W, W), bf),
            pltpu.VMEM((rows, groups * W), f32),
            pltpu.SemaphoreType.DMA((2,)),
            pltpu.SemaphoreType.DMA((half,)),
            pltpu.SemaphoreType.DMA((2,)),
            pltpu.SemaphoreType.DMA((2,)),
            pltpu.SemaphoreType.DMA((T * half,)),
            pltpu.SemaphoreType.DMA,
            pltpu.SemaphoreType.DMA((C,)),
            pltpu.SemaphoreType.DMA,
            pltpu.SemaphoreType.DMA((T, half)),
            pltpu.SemaphoreType.DMA((T, half)),
        ],
        compiler_params=pltpu.CompilerParams(
            collective_id=0, has_side_effects=True, vmem_limit_bytes=62 * 1024 * 1024
        ),
    )(raw_strain, fir_taps.reshape(1, TAPS), sources)
    return jnp.swapaxes(flat.reshape(STEPS, LAGS, step_len, rows), 1, 2)


def solution(mesh):
    C, T = mesh.shape["chan"], mesh.shape["tm"]
    return jax.shard_map(
        functools.partial(per_device, C, T),
        mesh=mesh,
        in_specs=(P("chan", "tm"), P(), P()),
        out_specs=P(None, "tm", None, "chan"),
        check_vma=False,
    )
```

time: 33.6 us -> 30.5 us (0.908)
  Pallas kernels: 32.5 us -> 29.4 us
    pallas_call x1, Pallas kernels: 32.5 us -> 29.4 us  [per_device(): pl.pallas_call(functools.partial(kernel, C, T, 1.0 / math.sqrt(total)), o...]
where the time goes in v1:
time: 30.5 us; the launch traced here: 30.4 us
  Pallas kernels  29.4 us (96%)
  local copies, waits for them, and re-layouts  0.97 us (3%)
    pallas_call x1, Pallas kernels, per_device(): pl.pallas_call(functools.partial(kernel, C, T, 1.0 / math.sqrt(total)), o...  29.4 us
    unnamed x1, local copies, waits for them, and re-layouts  0.97 us

profile of v1, /device:TPU:0, one launch (start us, length us, event | category | flops | bytes accessed | tf_op | source)
XLA Modules:
  0.0 30.4 jit_solution(15012480833204777049)
XLA Ops:
  0.0 29.4 %shard_map.37 = f32[2056,128]{1,0:T(8,128)S(1)} custom-call(bf16[128,8192]{1,0:T(8,128)(2,1)} %raw_ref.1, bf16[1,64]{1,0:T(2,128)(2,1)} %bitcast.5, s32[2,8]{1,0:T(2,128)} %src_hbm.1), custom_call_target="tpu_custom_call" | custom-call | tf_op jit(solution)/shard_map/pallas_call | solution.py:401
  29.4 1.0 %copy.5 = f32[2,4,257,128]{3,1,2,0:T(4,128)} copy(f32[2,4,257,128]{3,1,2,0:T(4,128)S(1)} %bitcast.4) | data formatting | bytes 2105344

commit v2 on v1

--- a/solution.py
+++ b/solution.py
@@ -16,7 +16,9 @@
 STEPS = 2
 W = 128
 SLAB = 8
-EARLY = 3
+LEAD = 1
+FIRST = 2
+EARLY = 4
 BLOCK = 1024
 LEFT = 256
 RIGHT = 128
@@ -36,7 +38,7 @@
 def kernel(
     C, T, scale,
     raw_ref, taps_hbm, src_hbm, out_ref,
-    taps_ref, src_ref, x_ref, dec_ref, hi_ref, lo_ref, white_ref, send1, recv1, recv2, rep_ref, shifted, acc_ref,
+    taps_ref, src_ref, x_ref, dec_ref, hi_ref, lo_ref, white_ref, send1, recv1, recv2, window_ref, shift_ref, shifted, acc_ref,
     small_sem, load_sem, halo_send, halo_recv, s1_sem, r1_sem, s2_sem, r2_sem, bulk_send, bulk_recv,
 ):
     c = lax.axis_index("chan")
@@ -136,15 +138,18 @@
         hi_ref[:, (b + 1) * W:(b + 2) * W] = hi
         lo_ref[:, (b + 1) * W:(b + 2) * W] = (mag - hi.astype(jnp.float32)).astype(jnp.bfloat16)
 
-    def chunk(b):
-        begin = LEFT - W + b * DECIM * W
-        d = nt(x_ref[:, begin:begin + (DECIM + 1) * W], ft)
-        dec_ref[:, b * W:(b + 1) * W] = d
-        put_mag(b, d)
+    def decimate(blocks):
+        begins = [LEFT - W + b * DECIM * W for b in blocks]
+        x = jnp.concatenate([x_ref[:, a:a + (DECIM + 1) * W] for a in begins], axis=0)
+        d = nt(x, ft)
+        for i, b in enumerate(blocks):
+            mine_d = d[i * rows:(i + 1) * rows]
+            dec_ref[:, b * W:(b + 1) * W] = mine_d
+            put_mag(b, mine_d)
 
     def first(g, i):
         k = g * half + i
-        dest = t * half + i
+        dest = i * T + t
         self_hit = (dest == c) & (g == t)
         remote = pltpu.make_async_remote_copy(
             src_ref=send1.at[k], dst_ref=recv1.at[c],
@@ -179,75 +184,100 @@
             device_id=(c, lax.rem(t + d, T)), device_id_type=MESH,
         )
 
-    def pair(p):
-        cols = slice(2 * p * W, (2 * p + 4) * W)
-        sums = nt(hi_ref[:, cols], band) + nt(lo_ref[:, cols], band)
+    def whiten(pairs):
+        cols = [slice(2 * p * W, (2 * p + 4) * W) for p in pairs]
+        sums = nt(jnp.concatenate([hi_ref[:, q] for q in cols], axis=0), band) + nt(
+            jnp.concatenate([lo_ref[:, q] for q in cols], axis=0), band
+        )
         level = sums / (2 * HALF_WIN + 1) + 1e-05
-        w = (dec_ref[:, 2 * p * W:2 * (p + 1) * W] / level).astype(jnp.bfloat16)
-        white_ref[:, pl.ds(aligned(mine + 2 * p * W), 2 * W)] = w
-        picked = jnp.dot(picks, w, preferred_element_type=jnp.float32)
-        for g in range(T):
-            send1[g * half + p] = jnp.concatenate(
-                [picked[g * SLAB:(g + 1) * SLAB, h * W:(h + 1) * W] for h in range(2)], axis=0
-            ).astype(jnp.bfloat16)
+        for i, p in enumerate(pairs):
+            d = dec_ref[:, 2 * p * W:2 * (p + 1) * W]
+            w = (d / level[i * rows:(i + 1) * rows]).astype(jnp.bfloat16)
+            white_ref[:, pl.ds(aligned(mine + 2 * p * W), 2 * W)] = w
+            picked = jnp.dot(picks, w, preferred_element_type=jnp.float32)
+            for g in range(T):
+                send1[g * half + p] = jnp.concatenate(
+                    [picked[g * SLAB:(g + 1) * SLAB, h * W:(h + 1) * W] for h in range(2)],
+                    axis=0,
+                ).astype(jnp.bfloat16)
 
     def all_bulk(i):
         for d in range(1, T):
             bulk(d, i).start()
 
+    def spread_out(pairs):
+        for p in pairs:
+            for g in range(T):
+                start_first(g, p)
+
     order = list(range(1, half - 1)) + [0, half - 1]
-    done = {0}
-    here = 0
-    for at, p in enumerate(order):
-        if p == 0:
-            @pl.when(t > 0)
-            def _():
-                to_right.wait_recv()
-
-            @pl.when(t < T - 1)
-            def _():
-                to_left.wait_recv()
-
-            chunk(0)
-            before = nt(x_ref[:, 0:LEFT], ft[:, 3 * W:5 * W])
-            keep = (t > 0) & (lax.broadcasted_iota(jnp.int32, (rows, W), 1) >= W - HALF_WIN)
-            put_mag(-1, jnp.where(keep, before, 0.0))
-            after = nt(x_ref[:, LEFT + raw_len - W:LEFT + raw_len + RIGHT], ft[:, 0:2 * W])
-            keep = (t < T - 1) & (lax.broadcasted_iota(jnp.int32, (rows, W), 1) < HALF_WIN)
-            put_mag(nb, jnp.where(keep, after, 0.0))
-        for b in range(2 * p - 1, min(2 * p + 3, nb)):
-            if b >= 0 and b not in done:
-                while here <= b // 2:
-                    loads[here].wait()
-                    here += 1
-                chunk(b)
-                done.add(b)
-        pair(p)
-        if at == 0:
-            pl.semaphore_wait(barrier, N - 1)
-
-            @pl.when(t < T - 1)
-            def _():
-                to_right.start()
-
-            @pl.when(t > 0)
-            def _():
-                to_left.start()
-
-            @pl.when(t == 0)
-            def _():
-                x_ref[:, 0:LEFT] = jnp.zeros((rows, LEFT), jnp.bfloat16)
-
-            @pl.when(t == T - 1)
-            def _():
-                x_ref[:, LEFT + raw_len:] = jnp.zeros((rows, RIGHT), jnp.bfloat16)
-
-        for g in range(T):
-            start_first(g, p)
-        if at < EARLY:
-            all_bulk(p)
+    lead = order[:LEAD]
+    inner = order[LEAD:half - 2]
+    edge = order[half - 2:]
+
+    pl.semaphore_wait(barrier, N - 1)
+
+    @pl.when(t < T - 1)
+    def _():
+        to_right.start()
+
+    @pl.when(t > 0)
+    def _():
+        to_left.start()
+
+    @pl.when(t == 0)
+    def _():
+        x_ref[:, 0:LEFT] = jnp.zeros((rows, LEFT), jnp.bfloat16)
+
+    @pl.when(t == T - 1)
+    def _():
+        x_ref[:, LEFT + raw_len:] = jnp.zeros((rows, RIGHT), jnp.bfloat16)
+
+    split = 2 * LEAD + 3
+    for i in range(-(-split // 2)):
+        loads[i].wait()
+    decimate(range(1, split))
+    whiten(lead)
+    spread_out(lead)
+    for p in lead:
+        all_bulk(p)
+    for i in range(-(-split // 2), half):
+        loads[i].wait()
+    decimate(range(split, nb))
+    whiten(inner)
+    spread_out(inner)
+    for p in order[LEAD:FIRST]:
+        all_bulk(p)
+
+    @pl.when(t > 0)
+    def _():
+        to_right.wait_recv()
+
+    @pl.when(t < T - 1)
+    def _():
+        to_left.wait_recv()
+
+    decimate([0])
+    past = nt(x_ref[:, 0:LEFT], ft[:, 3 * W:5 * W])
+    keep = (t > 0) & (lax.broadcasted_iota(jnp.int32, (rows, W), 1) >= W - HALF_WIN)
+    put_mag(-1, jnp.where(keep, past, 0.0))
+    after = nt(x_ref[:, LEFT + raw_len - W:LEFT + raw_len + RIGHT], ft[:, 0:2 * W])
+    keep = (t < T - 1) & (lax.broadcasted_iota(jnp.int32, (rows, W), 1) < HALF_WIN)
+    put_mag(nb, jnp.where(keep, after, 0.0))
+    whiten(edge)
+    spread_out(edge)
+    for p in order[FIRST:EARLY]:
+        all_bulk(p)
 
     shifted[0:W, :] = jnp.zeros((W, W), jnp.bfloat16)
+    lags = W // ns
+    tall = lags * step_len
+    tiles = tall // SLAB
+    group = SLAB // step_len
+    sample = lax.broadcasted_iota(jnp.int32, (2 * W, tiles * W), 0)
+    place = lax.broadcasted_iota(jnp.int32, (2 * W, tiles * W), 1)
+    shift = jnp.where(sample == W + place % W - place // W * group, 1.0, 0.0)
+    shift_ref[...] = shift.astype(jnp.bfloat16)
 
     def each(count, body):
         if count <= 16:
@@ -280,49 +310,54 @@
         all_bulk(i)
     pltpu.make_async_copy(recv2, recv2, r2_sem).wait()
 
-    lags = W // ns
-    tall = lags * step_len
-    tiles = tall // SLAB
-    group = SLAB // step_len
-    gathered = jnp.concatenate([recv2[j] for j in range(C)], axis=1)
+    gathered = jnp.concatenate([recv2[q % half * T + q // half] for q in range(C)], axis=1)
     spread_row = lax.broadcasted_iota(jnp.int32, (2 * STEPS * SLAB, 2 * SLAB), 0)
     spread_col = lax.broadcasted_iota(jnp.int32, (2 * STEPS * SLAB, 2 * SLAB), 1)
     wanted = (spread_row // (STEPS * SLAB)) * SLAB + (spread_row // SLAB % STEPS) * step_len + (
         spread_row % step_len
     )
     spread = jnp.where(spread_col == wanted, 1.0, 0.0).astype(jnp.bfloat16)
-    rep_ref[...] = jnp.dot(spread, gathered, preferred_element_type=jnp.float32)
+    rep = jnp.dot(spread, gathered, preferred_element_type=jnp.float32)
     low = lax.broadcasted_iota(jnp.int32, (SLAB, W), 0) // step_len
-    low_lane = lax.broadcasted_iota(jnp.int32, (SLAB, W), 1) - low
+    lane = lax.broadcasted_iota(jnp.int32, (SLAB, W), 1)
     zero = jnp.zeros((SLAB, W), jnp.float32)
-
-    def build(j, prev):
-        for h in range(2):
-            now = []
-            for step in range(STEPS):
-                top = (h * STEPS + step) * SLAB
-                x = rep_ref[top:top + SLAB, pl.ds(aligned(j * W), W)]
-                start = x
-                for k in range(1, group):
-                    start = jnp.where(low == k, pltpu.roll(x, k, 1), start)
-                for v in range(tiles):
-                    now.append(pltpu.roll(start, v * group, 1) if v else start)
-            put_shifted(aligned((2 * j + h + 1) * W), now, prev)
-            prev = tuple(now)
-        return prev
-
-    def put_shifted(at, now, prev):
-        z = jnp.concatenate(
-            [
-                jnp.where(low_lane >= (v % tiles) * group, now[v], prev[v])
-                for v in range(STEPS * tiles)
-            ],
-            axis=0,
-        )
-        shifted[pl.ds(at, W), :] = z.T.astype(jnp.bfloat16)
-
-    last = lax.fori_loop(0, C, build, (zero,) * (STEPS * tiles))
-    put_shifted(W + total, (zero,) * (STEPS * tiles), last)
+    before = [zero] * STEPS
+    turned = [[zero] * group] * STEPS
+    for q in range(2 * C + 1):
+        for step in range(STEPS):
+            if q < 2 * C:
+                top = (q % 2 * STEPS + step) * SLAB
+                x = rep[top:top + SLAB, q // 2 * W:(q // 2 + 1) * W]
+                turn = [x] + [pltpu.roll(x, k, 1) for k in range(1, group)]
+            else:
+                x, turn = zero, [zero] * group
+            for k in range(1, group):
+                x = jnp.where(
+                    low == k, jnp.where(lane >= k, turn[k], turned[step][k]), x
+                )
+            turned = turned[:step] + [turn] + turned[step + 1:]
+            at = (q * STEPS + step) * SLAB
+            window_ref[at:at + SLAB, 0:W] = before[step]
+            window_ref[at:at + SLAB, W:] = x
+            before[step] = x
+    batch = 12
+    for q in range(0, 2 * C + 1, batch):
+        count = min(batch, 2 * C + 1 - q)
+        span = STEPS * SLAB
+        moved = jnp.dot(
+            window_ref[q * span:(q + count) * span, :].astype(jnp.bfloat16), shift_ref[...],
+            preferred_element_type=jnp.float32,
+        )
+        for i in range(count):
+            z = jnp.concatenate(
+                [
+                    moved[(i * STEPS + step) * SLAB:(i * STEPS + step + 1) * SLAB, v * W:(v + 1) * W]
+                    for step in range(STEPS)
+                    for v in range(tiles)
+                ],
+                axis=0,
+            )
+            shifted[(q + i + 1) * W:(q + i + 2) * W, :] = z.T.astype(jnp.bfloat16)
 
     groups = 2 * HALF_LAG // lags + 1
 
@@ -418,7 +453,8 @@
             pltpu.VMEM((T * half + 1, 16, W), bf),
             pltpu.VMEM((C, 16, W), bf),
             pltpu.VMEM((C, 16, W), bf),
-            pltpu.VMEM((2 * STEPS * SLAB, C * W), f32),
+            pltpu.VMEM(((2 * C + 1) * STEPS * SLAB, 2 * W), f32),
+            pltpu.VMEM((2 * W, W // ns * step_len // SLAB * W), bf),
             pltpu.VMEM((total + 2 * W, W), bf),
             pltpu.VMEM((rows, groups * W), f32),
             pltpu.SemaphoreType.DMA((2,)),

time: 30.5 us -> 26.7 us (0.88)
  Pallas kernels: 29.4 us -> 25.5 us
    pallas_call x1, Pallas kernels: 29.4 us -> 25.5 us  [per_device(): pl.pallas_call(functools.partial(kernel, C, T, 1.0 / math.sqrt(total)), o...]
where the time goes in v2:
time: 26.7 us; the launch traced here: 26.5 us
  Pallas kernels  25.5 us (96%)
  local copies, waits for them, and re-layouts  0.97 us (4%)
    pallas_call x1, Pallas kernels, per_device(): pl.pallas_call(functools.partial(kernel, C, T, 1.0 / math.sqrt(total)), o...  25.5 us
    unnamed x1, local copies, waits for them, and re-layouts  0.97 us

profile of v2, /device:TPU:0, one launch (start us, length us, event | category | flops | bytes accessed | tf_op | source)
XLA Modules:
  0.0 26.5 jit_solution(3091940452123140548)
XLA Ops:
  0.0 25.5 %shard_map.37 = f32[2056,128]{1,0:T(8,128)S(1)} custom-call(bf16[128,8192]{1,0:T(8,128)(2,1)} %raw_ref.1, bf16[1,64]{1,0:T(2,128)(2,1)} %bitcast.5, s32[2,8]{1,0:T(2,128)} %src_hbm.1), custom_call_target="tpu_custom_call" | custom-call | tf_op jit(solution)/shard_map/pallas_call | solution.py:436
  25.5 1.0 %copy.5 = f32[2,4,257,128]{3,1,2,0:T(4,128)} copy(f32[2,4,257,128]{3,1,2,0:T(4,128)S(1)} %bitcast.4) | data formatting | bytes 2105344

commit v3 on v2

--- a/solution.py
+++ b/solution.py
@@ -16,9 +16,10 @@
 STEPS = 2
 W = 128
 SLAB = 8
-LEAD = 1
-FIRST = 2
-EARLY = 4
+LOCAL = 4
+LEAD = 2
+EAGER = True
+AHEAD = (2, 2, 4, 6)
 BLOCK = 1024
 LEFT = 256
 RIGHT = 128
@@ -38,32 +39,48 @@
 def kernel(
     C, T, scale,
     raw_ref, taps_hbm, src_hbm, out_ref,
-    taps_ref, src_ref, x_ref, dec_ref, hi_ref, lo_ref, white_ref, send1, recv1, recv2, window_ref, shift_ref, shifted, acc_ref,
-    small_sem, load_sem, halo_send, halo_recv, s1_sem, r1_sem, s2_sem, r2_sem, bulk_send, bulk_recv,
+    taps_ref, src_ref, praw_ref, x_ref, dec_ref, hi_ref, lo_ref, white_ref, send1, recv1, part, recv2, mixed, recv3, window_ref, shift_ref, shifted, acc_ref,
+    small_sem, load_sem, halo_send, halo_recv, s1_sem, r1_sem, s2_sem, r2_sem, s3_sem, r3_sem, bulk_send, bulk_recv,
 ):
     c = lax.axis_index("chan")
     t = lax.axis_index("tm")
-    N = C * T
     rows, raw_len = raw_ref.shape
     dec_len = raw_len // DECIM
     nb = dec_len // W
-    half = nb // ((T * nb) // C)
+    half = nb // 2
+    per = half // LOCAL
     step_len = src_hbm.shape[1] // T
     ns = STEPS * step_len
-    me = c * T + t
     total = T * dec_len
     mine = t * dec_len
 
     barrier = pltpu.get_barrier_semaphore()
 
-    def greet(d, _):
-        other = lax.rem(me + d, N)
+    Z = C // LOCAL
+    deck, l = c // LOCAL, lax.rem(c, LOCAL)
+    near = LOCAL * T
+    spot = l * T + t
+
+    def beside(d):
+        other = lax.rem(spot + d, near)
+        return other // T, lax.rem(other, T)
+
+    def along(d):
+        return lax.rem(deck + d, Z) * LOCAL + l, t
+
+    def greet_beside(d, _):
+        to_l, to_t = beside(d)
         pl.semaphore_signal(
-            barrier, inc=1, device_id=(other // T, lax.rem(other, T)), device_id_type=MESH
+            barrier, inc=1, device_id=(deck * LOCAL + to_l, to_t), device_id_type=MESH
         )
         return 0
 
-    lax.fori_loop(1, N, greet, 0)
+    def greet_along(d, _):
+        pl.semaphore_signal(barrier, inc=1, device_id=along(d), device_id_type=MESH)
+        return 0
+
+    lax.fori_loop(1, Z, greet_along, 0)
+    lax.fori_loop(1, near, greet_beside, 0)
 
     small = [
         pltpu.make_async_copy(taps_hbm, taps_ref, small_sem.at[0]),
@@ -82,6 +99,37 @@
         load.start()
         loads.append(load)
 
+    to_right = pltpu.make_async_remote_copy(
+        src_ref=raw_ref.at[:, pl.ds(raw_len - LEFT, LEFT)],
+        dst_ref=x_ref.at[:, pl.ds(0, LEFT)],
+        send_sem=halo_send.at[0], recv_sem=halo_recv.at[0],
+        device_id=(c, lax.rem(t + 1, T)), device_id_type=MESH,
+    )
+    to_left = pltpu.make_async_remote_copy(
+        src_ref=raw_ref.at[:, pl.ds(0, RIGHT)],
+        dst_ref=x_ref.at[:, pl.ds(LEFT + raw_len, RIGHT)],
+        send_sem=halo_send.at[1], recv_sem=halo_recv.at[1],
+        device_id=(c, lax.rem(t + T - 1, T)), device_id_type=MESH,
+    )
+
+    pl.semaphore_wait(barrier, near - 1 + Z - 1)
+
+    @pl.when(t < T - 1)
+    def _():
+        to_right.start()
+
+    @pl.when(t > 0)
+    def _():
+        to_left.start()
+
+    @pl.when(t == 0)
+    def _():
+        x_ref[:, 0:LEFT] = jnp.zeros((rows, LEFT), jnp.bfloat16)
+
+    @pl.when(t == T - 1)
+    def _():
+        x_ref[:, LEFT + raw_len:] = jnp.zeros((rows, RIGHT), jnp.bfloat16)
+
     span = lax.broadcasted_iota(jnp.int32, (2 * W, 4 * W), 1) - W - lax.broadcasted_iota(
         jnp.int32, (2 * W, 4 * W), 0
     )
@@ -119,19 +167,6 @@
                 picks = jnp.where(hit, 1.0, picks)
     picks = picks.astype(jnp.bfloat16)
 
-    to_right = pltpu.make_async_remote_copy(
-        src_ref=raw_ref.at[:, pl.ds(raw_len - LEFT, LEFT)],
-        dst_ref=x_ref.at[:, pl.ds(0, LEFT)],
-        send_sem=halo_send.at[0], recv_sem=halo_recv.at[0],
-        device_id=(c, lax.rem(t + 1, T)), device_id_type=MESH,
-    )
-    to_left = pltpu.make_async_remote_copy(
-        src_ref=raw_ref.at[:, pl.ds(0, RIGHT)],
-        dst_ref=x_ref.at[:, pl.ds(LEFT + raw_len, RIGHT)],
-        send_sem=halo_send.at[1], recv_sem=halo_recv.at[1],
-        device_id=(c, lax.rem(t + T - 1, T)), device_id_type=MESH,
-    )
-
     def put_mag(b, d):
         mag = jnp.abs(d)
         hi = mag.astype(jnp.bfloat16)
@@ -147,34 +182,27 @@
             dec_ref[:, b * W:(b + 1) * W] = mine_d
             put_mag(b, mine_d)
 
-    def first(g, i):
-        k = g * half + i
-        dest = i * T + t
-        self_hit = (dest == c) & (g == t)
-        remote = pltpu.make_async_remote_copy(
-            src_ref=send1.at[k], dst_ref=recv1.at[c],
-            send_sem=s1_sem.at[k], recv_sem=r1_sem,
-            device_id=(dest, g), device_id_type=MESH,
-        )
-        return self_hit, remote
-
-    def start_first(g, i):
-        self_hit, remote = first(g, i)
-
-        @pl.when(jnp.logical_not(self_hit))
-        def _():
-            remote.start()
-
-        @pl.when(self_hit)
-        def _():
-            pltpu.make_async_copy(send1.at[g * half + i], recv1.at[c], r1_sem).start()
-
-    def end_first(g, i):
-        self_hit, remote = first(g, i)
-
-        @pl.when(jnp.logical_not(self_hit))
-        def _():
-            remote.wait_send()
+    def first(d):
+        to_l, g = beside(d)
+        return pltpu.make_async_remote_copy(
+            src_ref=send1.at[g * LOCAL + to_l], dst_ref=recv1.at[t * LOCAL + l],
+            send_sem=s1_sem.at[d - 1], recv_sem=r1_sem,
+            device_id=(deck * LOCAL + to_l, g), device_id_type=MESH,
+        )
+
+    def second(d):
+        return pltpu.make_async_remote_copy(
+            src_ref=part, dst_ref=recv2.at[d - 1],
+            send_sem=s2_sem.at[d - 1], recv_sem=r2_sem,
+            device_id=along(d), device_id_type=MESH,
+        )
+
+    def third(d):
+        return pltpu.make_async_remote_copy(
+            src_ref=mixed, dst_ref=recv3.at[l],
+            send_sem=s3_sem.at[d - 1], recv_sem=r3_sem,
+            device_id=(deck * LOCAL + lax.rem(l + d, LOCAL), t), device_id_type=MESH,
+        )
 
     def bulk(d, i):
         cols = pl.ds(aligned(mine + i * 2 * W), 2 * W)
@@ -194,69 +222,117 @@
             d = dec_ref[:, 2 * p * W:2 * (p + 1) * W]
             w = (d / level[i * rows:(i + 1) * rows]).astype(jnp.bfloat16)
             white_ref[:, pl.ds(aligned(mine + 2 * p * W), 2 * W)] = w
-            picked = jnp.dot(picks, w, preferred_element_type=jnp.float32)
-            for g in range(T):
-                send1[g * half + p] = jnp.concatenate(
-                    [picked[g * SLAB:(g + 1) * SLAB, h * W:(h + 1) * W] for h in range(2)],
-                    axis=0,
-                ).astype(jnp.bfloat16)
 
     def all_bulk(i):
         for d in range(1, T):
             bulk(d, i).start()
 
-    def spread_out(pairs):
-        for p in pairs:
-            for g in range(T):
-                start_first(g, p)
+    def each(count, body):
+        if count <= 16:
+            for i in range(count):
+                body(i)
+            return
+
+        def step(i, _):
+            body(i)
+            return 0
+
+        lax.fori_loop(0, count, step, 0)
 
     order = list(range(1, half - 1)) + [0, half - 1]
     lead = order[:LEAD]
     inner = order[LEAD:half - 2]
     edge = order[half - 2:]
 
-    pl.semaphore_wait(barrier, N - 1)
+    def pick_raw(x):
+        return jnp.dot(picks, x, preferred_element_type=jnp.float32).astype(jnp.bfloat16)
+
+    ahead = (DECIM + 1) * W
+    many = T * SLAB
+    praw_ref[:, 0:ahead - LEFT] = jnp.zeros((many, ahead - LEFT), jnp.bfloat16)
+    praw_ref[:, ahead + raw_len + RIGHT:] = jnp.zeros((many, DECIM * W - RIGHT), jnp.bfloat16)
+    for i in range(half):
+        loads[i].wait()
+        praw_ref[:, ahead + i * seg:ahead + (i + 1) * seg] = pick_raw(
+            x_ref[:, LEFT + i * seg:LEFT + (i + 1) * seg]
+        )
+    made = {}
+
+    def filter_picks(blocks):
+        d = nt(
+            jnp.concatenate(
+                [praw_ref[:, a:a + ahead] for a in [(b + 1) * DECIM * W for b in blocks]], axis=0
+            ),
+            ft,
+        )
+        for i, b in enumerate(blocks):
+            mine_d = d[i * many:(i + 1) * many]
+            mag = jnp.abs(mine_d)
+            lane = lax.broadcasted_iota(jnp.int32, (many, W), 1)
+            if b < 0:
+                mag = jnp.where((t > 0) & (lane >= W - HALF_WIN), mag, 0.0)
+            if b == nb:
+                mag = jnp.where((t < T - 1) & (lane < HALF_WIN), mag, 0.0)
+            hi = mag.astype(jnp.bfloat16)
+            made[b] = mine_d, hi, (mag - hi.astype(jnp.float32)).astype(jnp.bfloat16)
+
+    narrow = band[0:W, 0:3 * W]
+    narrow = jnp.concatenate([narrow, narrow], axis=1)
+
+    def whiten_picks(pairs):
+        blocks = [b for p in pairs for b in (2 * p, 2 * p + 1)]
+        wide = jnp.concatenate(
+            [
+                jnp.concatenate([made[b + k][m] for m in (1, 2) for k in (-1, 0, 1)], axis=1)
+                for b in blocks
+            ],
+            axis=0,
+        )
+        level = nt(wide, narrow) / (2 * HALF_WIN + 1) + 1e-05
+        d = jnp.concatenate([made[b][0] for b in blocks], axis=0) / level
+        for i, p in enumerate(pairs):
+            at = p % per * 2 * SLAB
+            for g in range(T):
+                send1[g * LOCAL + p // per, at:at + 2 * SLAB] = jnp.concatenate(
+                    [
+                        d[q * many + g * SLAB:q * many + (g + 1) * SLAB]
+                        for q in (2 * i, 2 * i + 1)
+                    ],
+                    axis=0,
+                ).astype(jnp.bfloat16)
+
+    filter_picks(range(1, nb))
+    whiten_picks(range(1, half - 1))
+    split = 2 * LEAD + 3
+    if EAGER:
+        decimate(range(1, split))
+        whiten(lead)
+
+    @pl.when(t > 0)
+    def _():
+        to_right.wait_recv()
 
     @pl.when(t < T - 1)
     def _():
-        to_right.start()
-
-    @pl.when(t > 0)
-    def _():
-        to_left.start()
-
-    @pl.when(t == 0)
-    def _():
-        x_ref[:, 0:LEFT] = jnp.zeros((rows, LEFT), jnp.bfloat16)
-
-    @pl.when(t == T - 1)
-    def _():
-        x_ref[:, LEFT + raw_len:] = jnp.zeros((rows, RIGHT), jnp.bfloat16)
-
-    split = 2 * LEAD + 3
-    for i in range(-(-split // 2)):
-        loads[i].wait()
-    decimate(range(1, split))
-    whiten(lead)
-    spread_out(lead)
-    for p in lead:
+        to_left.wait_recv()
+
+    praw_ref[:, ahead - LEFT:ahead] = pick_raw(x_ref[:, 0:LEFT])
+    praw_ref[:, ahead + raw_len:ahead + raw_len + RIGHT] = pick_raw(x_ref[:, LEFT + raw_len:])
+    filter_picks([-1, 0, nb])
+    whiten_picks([0, half - 1])
+    each(near - 1, lambda d: first(d + 1).start())
+    pltpu.make_async_copy(
+        send1.at[t * LOCAL + l], recv1.at[t * LOCAL + l], r1_sem
+    ).start()
+    if not EAGER:
+        decimate(range(1, split))
+        whiten(lead)
+    for p in order[:AHEAD[0]]:
         all_bulk(p)
-    for i in range(-(-split // 2), half):
-        loads[i].wait()
     decimate(range(split, nb))
     whiten(inner)
-    spread_out(inner)
-    for p in order[LEAD:FIRST]:
+    for p in order[AHEAD[0]:AHEAD[1]]:
         all_bulk(p)
-
-    @pl.when(t > 0)
-    def _():
-        to_right.wait_recv()
-
-    @pl.when(t < T - 1)
-    def _():
-        to_left.wait_recv()
-
     decimate([0])
     past = nt(x_ref[:, 0:LEFT], ft[:, 3 * W:5 * W])
     keep = (t > 0) & (lax.broadcasted_iota(jnp.int32, (rows, W), 1) >= W - HALF_WIN)
@@ -265,8 +341,7 @@
     keep = (t < T - 1) & (lax.broadcasted_iota(jnp.int32, (rows, W), 1) < HALF_WIN)
     put_mag(nb, jnp.where(keep, after, 0.0))
     whiten(edge)
-    spread_out(edge)
-    for p in order[FIRST:EARLY]:
+    for p in order[AHEAD[1]:AHEAD[2]]:
         all_bulk(p)
 
     shifted[0:W, :] = jnp.zeros((W, W), jnp.bfloat16)
@@ -279,38 +354,35 @@
     shift = jnp.where(sample == W + place % W - place // W * group, 1.0, 0.0)
     shift_ref[...] = shift.astype(jnp.bfloat16)
 
-    def each(count, body):
-        if count <= 16:
-            for i in range(count):
-                body(i)
-            return
-
-        def step(i, _):
-            body(i)
-            return 0
-
-        lax.fori_loop(0, count, step, 0)
-
     pltpu.make_async_copy(recv1, recv1, r1_sem).wait()
-    summed = recv1[0].astype(jnp.float32)
-    for j in range(1, C):
-        summed = summed + recv1[j].astype(jnp.float32)
-    send1[T * half] = summed.astype(jnp.bfloat16)
-
-    def second(d):
-        return pltpu.make_async_remote_copy(
-            src_ref=send1.at[T * half], dst_ref=recv2.at[c],
-            send_sem=s2_sem.at[d], recv_sem=r2_sem,
-            device_id=(lax.rem(c + d + 1, C), t), device_id_type=MESH,
-        )
-
-    each(C - 1, lambda d: second(d).start())
-    pltpu.make_async_copy(send1.at[T * half], recv2.at[c], r2_sem).start()
-    for i in order[EARLY:]:
-        all_bulk(i)
+    for g in range(T):
+        summed = recv1[g * LOCAL].astype(jnp.float32)
+        for j in range(1, LOCAL):
+            summed = summed + recv1[g * LOCAL + j].astype(jnp.float32)
+        part[g] = summed.astype(jnp.bfloat16)
+    each(Z - 1, lambda d: second(d + 1).start())
+    for p in order[AHEAD[2]:AHEAD[3]]:
+        all_bulk(p)
     pltpu.make_async_copy(recv2, recv2, r2_sem).wait()
-
-    gathered = jnp.concatenate([recv2[q % half * T + q // half] for q in range(C)], axis=1)
+    for g in range(T):
+        summed = part[g].astype(jnp.float32)
+        for j in range(Z - 1):
+            summed = summed + recv2[j, g].astype(jnp.float32)
+        mixed[g] = summed.astype(jnp.bfloat16)
+    each(LOCAL - 1, lambda d: third(d + 1).start())
+    pltpu.make_async_copy(mixed, recv3.at[l], r3_sem).start()
+    for p in order[AHEAD[3]:]:
+        all_bulk(p)
+    pltpu.make_async_copy(recv3, recv3, r3_sem).wait()
+
+    gathered = jnp.concatenate(
+        [
+            recv3[p // per, g, p % per * 2 * SLAB:(p % per + 1) * 2 * SLAB]
+            for g in range(T)
+            for p in range(half)
+        ],
+        axis=1,
+    )
     spread_row = lax.broadcasted_iota(jnp.int32, (2 * STEPS * SLAB, 2 * SLAB), 0)
     spread_col = lax.broadcasted_iota(jnp.int32, (2 * STEPS * SLAB, 2 * SLAB), 1)
     wanted = (spread_row // (STEPS * SLAB)) * SLAB + (spread_row // SLAB % STEPS) * step_len + (
@@ -323,9 +395,9 @@
     zero = jnp.zeros((SLAB, W), jnp.float32)
     before = [zero] * STEPS
     turned = [[zero] * group] * STEPS
-    for q in range(2 * C + 1):
+    for q in range(T * nb + 1):
         for step in range(STEPS):
-            if q < 2 * C:
+            if q < T * nb:
                 top = (q % 2 * STEPS + step) * SLAB
                 x = rep[top:top + SLAB, q // 2 * W:(q // 2 + 1) * W]
                 turn = [x] + [pltpu.roll(x, k, 1) for k in range(1, group)]
@@ -341,8 +413,8 @@
             window_ref[at:at + SLAB, W:] = x
             before[step] = x
     batch = 12
-    for q in range(0, 2 * C + 1, batch):
-        count = min(batch, 2 * C + 1 - q)
+    for q in range(0, T * nb + 1, batch):
+        count = min(batch, T * nb + 1 - q)
         span = STEPS * SLAB
         moved = jnp.dot(
             window_ref[q * span:(q + count) * span, :].astype(jnp.bfloat16), shift_ref[...],
@@ -361,15 +433,23 @@
 
     groups = 2 * HALF_LAG // lags + 1
 
-    def products(n, count, fresh=False):
-        w = white_ref[:, pl.ds(aligned(n), count)]
+    def products(starts, count, fresh=False):
+        w = jnp.concatenate([white_ref[:, pl.ds(aligned(n), count)] for n in starts], axis=1)
         for k in range(0, groups, 2):
             b = jnp.concatenate(
                 [
-                    shifted[pl.ds(pl.multiple_of(n + 2 * HALF_LAG - lags * m, 16), count), :]
-                    for m in range(k, min(k + 2, groups))
+                    jnp.concatenate(
+                        [
+                            shifted[
+                                pl.ds(pl.multiple_of(n + 2 * HALF_LAG - lags * m, 16), count), :
+                            ]
+                            for m in range(k, min(k + 2, groups))
+                        ],
+                        axis=1,
+                    )
+                    for n in starts
                 ],
-                axis=1,
+                axis=0,
             )
             out = jnp.dot(w, b, preferred_element_type=jnp.float32)
             cols = slice(k * W, k * W + b.shape[1])
@@ -378,21 +458,21 @@
             else:
                 acc_ref[:, cols] += out
 
-    block = min(BLOCK, dec_len)
-    for q in range(dec_len // block):
-        products(mine + q * block, block, q == 0)
-
-    def arrive(d, i):
-        at = lax.rem(t + T - d, T) * dec_len + i * 2 * W
-        cols = pl.ds(aligned(at), 2 * W)
-        pltpu.make_async_copy(
-            white_ref.at[:, cols], white_ref.at[:, cols], bulk_recv.at[d - 1, i]
-        ).wait()
-        products(at, 2 * W)
+    for q in range(0, dec_len, min(BLOCK, dec_len)):
+        products([mine + q], min(BLOCK, dec_len), q == 0)
 
     def arrivals(d, _):
-        for i in order:
-            arrive(d, i)
+        begin = lax.rem(t + T - d, T) * dec_len
+        for pairs in (order[:half - 2], edge):
+            for i in pairs:
+                cols = pl.ds(aligned(begin + i * 2 * W), 2 * W)
+                pltpu.make_async_copy(
+                    white_ref.at[:, cols], white_ref.at[:, cols], bulk_recv.at[d - 1, i]
+                ).wait()
+            if pairs[-1] - pairs[0] == len(pairs) - 1:
+                products([begin + pairs[0] * 2 * W], len(pairs) * 2 * W)
+            else:
+                products([begin + i * 2 * W for i in pairs], 2 * W)
         return 0
 
     if T == 2:
@@ -415,9 +495,9 @@
     def _():
         to_left.wait_send()
 
-    for g in range(T):
-        each(half, lambda i: end_first(g, i))
-    each(C - 1, lambda d: second(d).wait_send())
+    each(near - 1, lambda d: first(d + 1).wait_send())
+    each(Z - 1, lambda d: second(d + 1).wait_send())
+    each(LOCAL - 1, lambda d: third(d + 1).wait_send())
     for d in range(1, T):
         for i in range(half):
             bulk(d, i).wait_send()
@@ -427,7 +507,8 @@
     rows, raw_len = raw_strain.shape
     dec_len = raw_len // DECIM
     nb = dec_len // W
-    half = nb * C // (T * nb)
+    half = nb // 2
+    tall = half // LOCAL * 2 * SLAB
     step_len = sources.shape[1] // T
     ns = STEPS * step_len
     total = T * dec_len
@@ -445,15 +526,19 @@
         scratch_shapes=[
             pltpu.VMEM((1, TAPS), bf),
             pltpu.SMEM(sources.shape, jnp.int32),
+            pltpu.VMEM((T * SLAB, raw_len + (2 * DECIM + 1) * W), bf),
             pltpu.VMEM((rows, LEFT + raw_len + RIGHT), bf),
             pltpu.VMEM((rows, dec_len), f32),
             pltpu.VMEM((rows, dec_len + 2 * W), bf),
             pltpu.VMEM((rows, dec_len + 2 * W), bf),
             pltpu.VMEM((rows, total), bf),
-            pltpu.VMEM((T * half + 1, 16, W), bf),
-            pltpu.VMEM((C, 16, W), bf),
-            pltpu.VMEM((C, 16, W), bf),
-            pltpu.VMEM(((2 * C + 1) * STEPS * SLAB, 2 * W), f32),
+            pltpu.VMEM((LOCAL * T, tall, W), bf),
+            pltpu.VMEM((LOCAL * T, tall, W), bf),
+            pltpu.VMEM((T, tall, W), bf),
+            pltpu.VMEM((C // LOCAL - 1, T, tall, W), bf),
+            pltpu.VMEM((T, tall, W), bf),
+            pltpu.VMEM((LOCAL, T, tall, W), bf),
+            pltpu.VMEM(((T * nb + 1) * STEPS * SLAB, 2 * W), f32),
             pltpu.VMEM((2 * W, W // ns * step_len // SLAB * W), bf),
             pltpu.VMEM((total + 2 * W, W), bf),
             pltpu.VMEM((rows, groups * W), f32),
@@ -461,9 +546,11 @@
             pltpu.SemaphoreType.DMA((half,)),
             pltpu.SemaphoreType.DMA((2,)),
             pltpu.SemaphoreType.DMA((2,)),
-            pltpu.SemaphoreType.DMA((T * half,)),
+            pltpu.SemaphoreType.DMA((LOCAL * T - 1,)),
             pltpu.SemaphoreType.DMA,
-            pltpu.SemaphoreType.DMA((C,)),
+            pltpu.SemaphoreType.DMA((C // LOCAL - 1,)),
+            pltpu.SemaphoreType.DMA,
+            pltpu.SemaphoreType.DMA((LOCAL - 1,)),
             pltpu.SemaphoreType.DMA,
             pltpu.SemaphoreType.DMA((T, half)),
             pltpu.SemaphoreType.DMA((T, half)),

time: 26.7 us -> 25.4 us (0.951)
  Pallas kernels: 25.5 us -> 24.3 us
    pallas_call x1, Pallas kernels: 25.5 us -> 24.3 us  [per_device(): pl.pallas_call(functools.partial(kernel, C, T, 1.0 / math.sqrt(total)), o...]
where the time goes in v3:
time: 25.4 us; the launch traced here: 25.3 us
  Pallas kernels  24.3 us (96%)
  local copies, waits for them, and re-layouts  0.97 us (4%)
    pallas_call x1, Pallas kernels, per_device(): pl.pallas_call(functools.partial(kernel, C, T, 1.0 / math.sqrt(total)), o...  24.3 us
    unnamed x1, local copies, waits for them, and re-layouts  0.97 us

profile of v3, /device:TPU:0, one launch (start us, length us, event | category | flops | bytes accessed | tf_op | source)
XLA Modules:
  0.0 25.3 jit_solution(13139056902222615146)
XLA Ops:
  0.0 24.3 %shard_map.37 = f32[2056,128]{1,0:T(8,128)S(1)} custom-call(bf16[128,8192]{1,0:T(8,128)(2,1)} %raw_ref.1, bf16[1,64]{1,0:T(2,128)(2,1)} %bitcast.5, s32[2,8]{1,0:T(2,128)} %src_hbm.1), custom_call_target="tpu_custom_call" | custom-call | tf_op jit(solution)/shard_map/pallas_call | solution.py:517
  24.3 1.0 %copy.5 = f32[2,4,257,128]{3,1,2,0:T(4,128)} copy(f32[2,4,257,128]{3,1,2,0:T(4,128)S(1)} %bitcast.4) | data formatting | bytes 2105344

commit v4 on v3

--- a/solution.py
+++ b/solution.py
@@ -17,9 +17,9 @@
 W = 128
 SLAB = 8
 LOCAL = 4
-LEAD = 2
-EAGER = True
-AHEAD = (2, 2, 4, 6)
+LEAD = 1
+MARGIN = 384
+AHEAD = (1, 2, 4, 6)
 BLOCK = 1024
 LEFT = 256
 RIGHT = 128
@@ -39,8 +39,8 @@
 def kernel(
     C, T, scale,
     raw_ref, taps_hbm, src_hbm, out_ref,
-    taps_ref, src_ref, praw_ref, x_ref, dec_ref, hi_ref, lo_ref, white_ref, send1, recv1, part, recv2, mixed, recv3, window_ref, shift_ref, shifted, acc_ref,
-    small_sem, load_sem, halo_send, halo_recv, s1_sem, r1_sem, s2_sem, r2_sem, s3_sem, r3_sem, bulk_send, bulk_recv,
+    taps_ref, src_ref, praw_ref, x_ref, dec_ref, hi_ref, lo_ref, white_ref, send0, recv0, send1, recv1, part, recv2, mixed, recv3, window_ref, shift_ref, shifted, acc_ref,
+    small_sem, load_sem, halo_send, halo_recv, s0_sem, r0_sem, s1_sem, r1_sem, s2_sem, r2_sem, s3_sem, r3_sem, bulk_send, bulk_recv,
 ):
     c = lax.axis_index("chan")
     t = lax.axis_index("tm")
@@ -245,94 +245,120 @@
     edge = order[half - 2:]
 
     def pick_raw(x):
-        return jnp.dot(picks, x, preferred_element_type=jnp.float32).astype(jnp.bfloat16)
+        return jnp.dot(picks, x, preferred_element_type=jnp.float32)
+
+    def split_mag(d):
+        mag = jnp.abs(d)
+        hi = mag.astype(jnp.bfloat16)
+        return hi, (mag - hi.astype(jnp.float32)).astype(jnp.bfloat16)
+
+    narrow = band[0:W, 0:3 * W]
+    narrow = jnp.concatenate([narrow, narrow], axis=1)
+
+    def divide(d, wide):
+        return d / (nt(wide, narrow) / (2 * HALF_WIN + 1) + 1e-05)
 
     ahead = (DECIM + 1) * W
     many = T * SLAB
-    praw_ref[:, 0:ahead - LEFT] = jnp.zeros((many, ahead - LEFT), jnp.bfloat16)
-    praw_ref[:, ahead + raw_len + RIGHT:] = jnp.zeros((many, DECIM * W - RIGHT), jnp.bfloat16)
+    praw_ref[:, 0:ahead] = jnp.zeros((many, ahead), jnp.bfloat16)
     for i in range(half):
         loads[i].wait()
-        praw_ref[:, ahead + i * seg:ahead + (i + 1) * seg] = pick_raw(
-            x_ref[:, LEFT + i * seg:LEFT + (i + 1) * seg]
-        )
-    made = {}
-
-    def filter_picks(blocks):
-        d = nt(
-            jnp.concatenate(
-                [praw_ref[:, a:a + ahead] for a in [(b + 1) * DECIM * W for b in blocks]], axis=0
-            ),
-            ft,
-        )
-        for i, b in enumerate(blocks):
-            mine_d = d[i * many:(i + 1) * many]
-            mag = jnp.abs(mine_d)
-            lane = lax.broadcasted_iota(jnp.int32, (many, W), 1)
-            if b < 0:
-                mag = jnp.where((t > 0) & (lane >= W - HALF_WIN), mag, 0.0)
-            if b == nb:
-                mag = jnp.where((t < T - 1) & (lane < HALF_WIN), mag, 0.0)
-            hi = mag.astype(jnp.bfloat16)
-            made[b] = mine_d, hi, (mag - hi.astype(jnp.float32)).astype(jnp.bfloat16)
-
-    narrow = band[0:W, 0:3 * W]
-    narrow = jnp.concatenate([narrow, narrow], axis=1)
-
-    def whiten_picks(pairs):
-        blocks = [b for p in pairs for b in (2 * p, 2 * p + 1)]
-        wide = jnp.concatenate(
-            [
-                jnp.concatenate([made[b + k][m] for m in (1, 2) for k in (-1, 0, 1)], axis=1)
-                for b in blocks
-            ],
-            axis=0,
-        )
-        level = nt(wide, narrow) / (2 * HALF_WIN + 1) + 1e-05
-        d = jnp.concatenate([made[b][0] for b in blocks], axis=0) / level
-        for i, p in enumerate(pairs):
-            at = p % per * 2 * SLAB
-            for g in range(T):
-                send1[g * LOCAL + p // per, at:at + 2 * SLAB] = jnp.concatenate(
-                    [
-                        d[q * many + g * SLAB:q * many + (g + 1) * SLAB]
-                        for q in (2 * i, 2 * i + 1)
-                    ],
-                    axis=0,
-                ).astype(jnp.bfloat16)
-
-    filter_picks(range(1, nb))
-    whiten_picks(range(1, half - 1))
-    split = 2 * LEAD + 3
-    if EAGER:
-        decimate(range(1, split))
-        whiten(lead)
-
-    @pl.when(t > 0)
-    def _():
-        to_right.wait_recv()
-
-    @pl.when(t < T - 1)
-    def _():
-        to_left.wait_recv()
-
-    praw_ref[:, ahead - LEFT:ahead] = pick_raw(x_ref[:, 0:LEFT])
-    praw_ref[:, ahead + raw_len:ahead + raw_len + RIGHT] = pick_raw(x_ref[:, LEFT + raw_len:])
-    filter_picks([-1, 0, nb])
-    whiten_picks([0, half - 1])
+        x = pick_raw(x_ref[:, LEFT + i * seg:LEFT + (i + 1) * seg])
+        praw_ref[:, ahead + i * seg:ahead + (i + 1) * seg] = x.astype(jnp.bfloat16)
+        for kind, which, begin in ((0, half - 1, seg - MARGIN), (1, 0, 0)):
+            if i == which:
+                for g in range(T):
+                    send0[kind, g] = jnp.concatenate(
+                        [
+                            x[g * SLAB:(g + 1) * SLAB, begin + k * W:begin + (k + 1) * W]
+                            for k in range(MARGIN // W)
+                        ]
+                        + [jnp.zeros((SLAB, W), jnp.float32)],
+                        axis=0,
+                    ).astype(jnp.bfloat16)
+
+    def outer(kind, e, g):
+        to_l = e * (LOCAL - 1)
+        slot = jnp.where(kind == 0, t, t - 1)
+        inside = t < T - 1 if kind == 0 else t > 0
+        same = (to_l == l) & (g == t)
+        copy = pltpu.make_async_remote_copy(
+            src_ref=send0.at[kind, g], dst_ref=recv0.at[kind, slot, l],
+            send_sem=s0_sem.at[kind, e, g], recv_sem=r0_sem,
+            device_id=(deck * LOCAL + to_l, g), device_id_type=MESH,
+        )
+        own = pltpu.make_async_copy(send0.at[kind, g], recv0.at[kind, slot, l], r0_sem)
+        return inside & jnp.logical_not(same), inside & same, copy, own
+
+    outers = [(kind, e, g) for kind in range(2) for e in range(2) for g in range(T)]
+
+    def start_outer(kind, e, g):
+        away, here, copy, own = outer(kind, e, g)
+
+        @pl.when(away)
+        def _():
+            copy.start()
+
+        @pl.when(here)
+        def _():
+            own.start()
+
+    def end_outer(kind, e, g):
+        away, here, copy, own = outer(kind, e, g)
+
+        @pl.when(away)
+        def _():
+            copy.wait_send()
+
+    for which in outers:
+        start_outer(*which)
+
+    d = nt(
+        jnp.concatenate(
+            [praw_ref[:, a:a + ahead] for a in [(b + 1) * DECIM * W for b in range(nb)]], axis=0
+        ),
+        ft,
+    )
+    none = jnp.zeros((many, W), jnp.bfloat16)
+    mags = [jnp.concatenate([none, m, none], axis=0) for m in split_mag(d)]
+    d = divide(
+        d,
+        jnp.concatenate(
+            [m[k * many:(k + nb) * many] for m in mags for k in range(3)], axis=1
+        ),
+    )
+    for p in range(half):
+        at = p % per * 2 * SLAB
+        for g in range(T):
+            send1[g * LOCAL + p // per, at:at + 2 * SLAB] = jnp.concatenate(
+                [
+                    d[q * many + g * SLAB:q * many + (g + 1) * SLAB]
+                    for q in (2 * p, 2 * p + 1)
+                ],
+                axis=0,
+            ).astype(jnp.bfloat16)
     each(near - 1, lambda d: first(d + 1).start())
     pltpu.make_async_copy(
         send1.at[t * LOCAL + l], recv1.at[t * LOCAL + l], r1_sem
     ).start()
-    if not EAGER:
-        decimate(range(1, split))
-        whiten(lead)
+    split = 2 * LEAD + 3
+    decimate(range(1, split))
+    whiten(lead)
     for p in order[:AHEAD[0]]:
         all_bulk(p)
     decimate(range(split, nb))
     whiten(inner)
     for p in order[AHEAD[0]:AHEAD[1]]:
         all_bulk(p)
+
+    @pl.when(t > 0)
+    def _():
+        to_right.wait_recv()
+
+    @pl.when(t < T - 1)
+    def _():
+        to_left.wait_recv()
+
     decimate([0])
     past = nt(x_ref[:, 0:LEFT], ft[:, 3 * W:5 * W])
     keep = (t > 0) & (lax.broadcasted_iota(jnp.int32, (rows, W), 1) >= W - HALF_WIN)
@@ -360,6 +386,52 @@
         for j in range(1, LOCAL):
             summed = summed + recv1[g * LOCAL + j].astype(jnp.float32)
         part[g] = summed.astype(jnp.bfloat16)
+
+    @pl.when((l == 0) | (l == LOCAL - 1))
+    def _():
+        pltpu.make_async_copy(recv0, recv0, r0_sem).wait()
+        row = lax.broadcasted_iota(jnp.int32, (2 * SLAB, W), 0)
+        lane = lax.broadcasted_iota(jnp.int32, (2 * SLAB, W), 1)
+        blank = jnp.zeros((SLAB, W), jnp.float32)
+        for g in range(T - 1):
+            tiles = []
+            for kind in range(2):
+                summed = recv0[kind, g, 0].astype(jnp.float32)
+                for j in range(1, LOCAL):
+                    summed = summed + recv0[kind, g, j].astype(jnp.float32)
+                tiles += [summed[k * SLAB:(k + 1) * SLAB] for k in range(MARGIN // W)]
+            raws = [[blank, blank] + tiles[0:3], tiles[2:6] + [blank]]
+            d = nt(
+                jnp.concatenate(
+                    [jnp.concatenate(r, axis=1) for r in raws], axis=0
+                ).astype(jnp.bfloat16),
+                ft,
+            )
+            wide = []
+            for m in split_mag(d):
+                m = m.astype(jnp.float32)
+                left, right = m[0:SLAB], m[SLAB:]
+                wide += [
+                    jnp.concatenate(pair, axis=0)
+                    for pair in ((blank, left), (left, right), (right, blank))
+                ]
+            d = divide(d, jnp.concatenate(wide, axis=1).astype(jnp.bfloat16))
+            swap = jnp.concatenate([d[SLAB:], d[0:SLAB]], axis=0)
+
+            @pl.when(l == LOCAL - 1)
+            def _():
+                old = part[g, 2 * SLAB * (per - 1):2 * SLAB * per].astype(jnp.float32)
+                edge_row = (row >= SLAB) & (lane >= W - HALF_WIN)
+                part[g, 2 * SLAB * (per - 1):2 * SLAB * per] = jnp.where(
+                    edge_row, swap, old
+                ).astype(jnp.bfloat16)
+
+            @pl.when(l == 0)
+            def _():
+                old = part[g + 1, 0:2 * SLAB].astype(jnp.float32)
+                edge_row = (row < SLAB) & (lane < HALF_WIN + TAPS // DECIM)
+                part[g + 1, 0:2 * SLAB] = jnp.where(edge_row, swap, old).astype(jnp.bfloat16)
+
     each(Z - 1, lambda d: second(d + 1).start())
     for p in order[AHEAD[2]:AHEAD[3]]:
         all_bulk(p)
@@ -495,6 +567,8 @@
     def _():
         to_left.wait_send()
 
+    for which in outers:
+        end_outer(*which)
     each(near - 1, lambda d: first(d + 1).wait_send())
     each(Z - 1, lambda d: second(d + 1).wait_send())
     each(LOCAL - 1, lambda d: third(d + 1).wait_send())
@@ -509,6 +583,7 @@
     nb = dec_len // W
     half = nb // 2
     tall = half // LOCAL * 2 * SLAB
+    margin = (MARGIN // W + 1) * SLAB
     step_len = sources.shape[1] // T
     ns = STEPS * step_len
     total = T * dec_len
@@ -532,6 +607,8 @@
             pltpu.VMEM((rows, dec_len + 2 * W), bf),
             pltpu.VMEM((rows, dec_len + 2 * W), bf),
             pltpu.VMEM((rows, total), bf),
+            pltpu.VMEM((2, T, margin, W), bf),
+            pltpu.VMEM((2, T - 1, LOCAL, margin, W), bf),
             pltpu.VMEM((LOCAL * T, tall, W), bf),
             pltpu.VMEM((LOCAL * T, tall, W), bf),
             pltpu.VMEM((T, tall, W), bf),
@@ -546,6 +623,8 @@
             pltpu.SemaphoreType.DMA((half,)),
             pltpu.SemaphoreType.DMA((2,)),
             pltpu.SemaphoreType.DMA((2,)),
+            pltpu.SemaphoreType.DMA((2, 2, T)),
+            pltpu.SemaphoreType.DMA,
             pltpu.SemaphoreType.DMA((LOCAL * T - 1,)),
             pltpu.SemaphoreType.DMA,
             pltpu.SemaphoreType.DMA((C // LOCAL - 1,)),

time: 25.4 us -> 24 us (0.945)
  Pallas kernels: 24.3 us -> 22.8 us
    pallas_call x1, Pallas kernels: 24.3 us -> 22.8 us  [per_device(): pl.pallas_call(functools.partial(kernel, C, T, 1.0 / math.sqrt(total)), o...]
where the time goes in v4:
time: 24 us; the launch traced here: 23.8 us
  Pallas kernels  22.8 us (95%)
  local copies, waits for them, and re-layouts  0.97 us (4%)
    pallas_call x1, Pallas kernels, per_device(): pl.pallas_call(functools.partial(kernel, C, T, 1.0 / math.sqrt(total)), o...  22.8 us
    unnamed x1, local copies, waits for them, and re-layouts  0.97 us

profile of v4, /device:TPU:0, one launch (start us, length us, event | category | flops | bytes accessed | tf_op | source)
XLA Modules:
  0.0 23.8 jit_solution(8554670024219092789)
XLA Ops:
  0.0 22.8 %shard_map.37 = f32[2056,128]{1,0:T(8,128)S(1)} custom-call(bf16[128,8192]{1,0:T(8,128)(2,1)} %raw_ref.1, bf16[1,64]{1,0:T(2,128)(2,1)} %bitcast.5, s32[2,8]{1,0:T(2,128)} %src_hbm.1), custom_call_target="tpu_custom_call" | custom-call | tf_op jit(solution)/shard_map/pallas_call | solution.py:592
  22.9 1.0 %copy.5 = f32[2,4,257,128]{3,1,2,0:T(4,128)} copy(f32[2,4,257,128]{3,1,2,0:T(4,128)S(1)} %bitcast.4) | data formatting | bytes 2105344

commit v5 on v4

--- a/solution.py
+++ b/solution.py
@@ -19,6 +19,7 @@
 LOCAL = 4
 LEAD = 1
 MARGIN = 384
+PRE = 1
 AHEAD = (1, 2, 4, 6)
 BLOCK = 1024
 LEFT = 256
@@ -258,11 +259,21 @@
     def divide(d, wide):
         return d / (nt(wide, narrow) / (2 * HALF_WIN + 1) + 1e-05)
 
+    split = 2 * LEAD + 3
+    soon = -(-split // 2)
+    for i in range(soon):
+        loads[i].wait()
+    decimate(range(1, split))
+    whiten(lead)
+    for p in order[:PRE]:
+        all_bulk(p)
+
     ahead = (DECIM + 1) * W
     many = T * SLAB
     praw_ref[:, 0:ahead] = jnp.zeros((many, ahead), jnp.bfloat16)
     for i in range(half):
-        loads[i].wait()
+        if i >= soon:
+            loads[i].wait()
         x = pick_raw(x_ref[:, LEFT + i * seg:LEFT + (i + 1) * seg])
         praw_ref[:, ahead + i * seg:ahead + (i + 1) * seg] = x.astype(jnp.bfloat16)
         for kind, which, begin in ((0, half - 1, seg - MARGIN), (1, 0, 0)):
@@ -341,10 +352,7 @@
     pltpu.make_async_copy(
         send1.at[t * LOCAL + l], recv1.at[t * LOCAL + l], r1_sem
     ).start()
-    split = 2 * LEAD + 3
-    decimate(range(1, split))
-    whiten(lead)
-    for p in order[:AHEAD[0]]:
+    for p in order[PRE:AHEAD[0]]:
         all_bulk(p)
     decimate(range(split, nb))
     whiten(inner)

time: 24 us -> 23.4 us (0.975)
  Pallas kernels: 22.8 us -> 22.3 us
    pallas_call x1, Pallas kernels: 22.8 us -> 22.3 us  [per_device(): pl.pallas_call(functools.partial(kernel, C, T, 1.0 / math.sqrt(total)), o...]
where the time goes in v5:
time: 23.4 us; the launch traced here: 23.3 us
  Pallas kernels  22.3 us (95%)
  local copies, waits for them, and re-layouts  0.97 us (4%)
    pallas_call x1, Pallas kernels, per_device(): pl.pallas_call(functools.partial(kernel, C, T, 1.0 / math.sqrt(total)), o...  22.3 us
    unnamed x1, local copies, waits for them, and re-layouts  0.97 us

profile of v5, /device:TPU:0, one launch (start us, length us, event | category | flops | bytes accessed | tf_op | source)
XLA Modules:
  0.0 23.3 jit_solution(16476915901399205769)
XLA Ops:
  0.0 22.3 %shard_map.37 = f32[2056,128]{1,0:T(8,128)S(1)} custom-call(bf16[128,8192]{1,0:T(8,128)(2,1)} %raw_ref.1, bf16[1,64]{1,0:T(2,128)(2,1)} %bitcast.5, s32[2,8]{1,0:T(2,128)} %src_hbm.1), custom_call_target="tpu_custom_call" | custom-call | tf_op jit(solution)/shard_map/pallas_call | solution.py:600
  22.3 1.0 %copy.5 = f32[2,4,257,128]{3,1,2,0:T(4,128)} copy(f32[2,4,257,128]{3,1,2,0:T(4,128)S(1)} %bitcast.4) | data formatting | bytes 2105344

commit v6 on v5

--- a/solution.py
+++ b/solution.py
@@ -40,7 +40,7 @@
 def kernel(
     C, T, scale,
     raw_ref, taps_hbm, src_hbm, out_ref,
-    taps_ref, src_ref, praw_ref, x_ref, dec_ref, hi_ref, lo_ref, white_ref, send0, recv0, send1, recv1, part, recv2, mixed, recv3, window_ref, shift_ref, shifted, acc_ref,
+    taps_ref, src_ref, praw_ref, x_ref, dec_ref, hi_ref, lo_ref, white_ref, send0, recv0, send1, recv1, part, recv2, mixed, recv3, window_ref, shift_ref, shifted, acc_ref, line_ref, far_ref,
     small_sem, load_sem, halo_send, halo_recv, s0_sem, r0_sem, s1_sem, r1_sem, s2_sem, r2_sem, s3_sem, r3_sem, bulk_send, bulk_recv,
 ):
     c = lax.axis_index("chan")
@@ -113,16 +113,6 @@
         device_id=(c, lax.rem(t + T - 1, T)), device_id_type=MESH,
     )
 
-    pl.semaphore_wait(barrier, near - 1 + Z - 1)
-
-    @pl.when(t < T - 1)
-    def _():
-        to_right.start()
-
-    @pl.when(t > 0)
-    def _():
-        to_left.start()
-
     @pl.when(t == 0)
     def _():
         x_ref[:, 0:LEFT] = jnp.zeros((rows, LEFT), jnp.bfloat16)
@@ -265,6 +255,8 @@
         loads[i].wait()
     decimate(range(1, split))
     whiten(lead)
+    pl.semaphore_wait(barrier, near - 1 + Z - 1)
+
     for p in order[:PRE]:
         all_bulk(p)
 
@@ -352,29 +344,20 @@
     pltpu.make_async_copy(
         send1.at[t * LOCAL + l], recv1.at[t * LOCAL + l], r1_sem
     ).start()
+    @pl.when(t < T - 1)
+    def _():
+        to_right.start()
+
+    @pl.when(t > 0)
+    def _():
+        to_left.start()
+
     for p in order[PRE:AHEAD[0]]:
         all_bulk(p)
     decimate(range(split, nb))
     whiten(inner)
     for p in order[AHEAD[0]:AHEAD[1]]:
         all_bulk(p)
-
-    @pl.when(t > 0)
-    def _():
-        to_right.wait_recv()
-
-    @pl.when(t < T - 1)
-    def _():
-        to_left.wait_recv()
-
-    decimate([0])
-    past = nt(x_ref[:, 0:LEFT], ft[:, 3 * W:5 * W])
-    keep = (t > 0) & (lax.broadcasted_iota(jnp.int32, (rows, W), 1) >= W - HALF_WIN)
-    put_mag(-1, jnp.where(keep, past, 0.0))
-    after = nt(x_ref[:, LEFT + raw_len - W:LEFT + raw_len + RIGHT], ft[:, 0:2 * W])
-    keep = (t < T - 1) & (lax.broadcasted_iota(jnp.int32, (rows, W), 1) < HALF_WIN)
-    put_mag(nb, jnp.where(keep, after, 0.0))
-    whiten(edge)
     for p in order[AHEAD[1]:AHEAD[2]]:
         all_bulk(p)
 
@@ -443,6 +426,7 @@
     each(Z - 1, lambda d: second(d + 1).start())
     for p in order[AHEAD[2]:AHEAD[3]]:
         all_bulk(p)
+
     pltpu.make_async_copy(recv2, recv2, r2_sem).wait()
     for g in range(T):
         summed = part[g].astype(jnp.float32)
@@ -451,6 +435,22 @@
         mixed[g] = summed.astype(jnp.bfloat16)
     each(LOCAL - 1, lambda d: third(d + 1).start())
     pltpu.make_async_copy(mixed, recv3.at[l], r3_sem).start()
+    @pl.when(t > 0)
+    def _():
+        to_right.wait_recv()
+
+    @pl.when(t < T - 1)
+    def _():
+        to_left.wait_recv()
+
+    decimate([0])
+    past = nt(x_ref[:, 0:LEFT], ft[:, 3 * W:5 * W])
+    keep = (t > 0) & (lax.broadcasted_iota(jnp.int32, (rows, W), 1) >= W - HALF_WIN)
+    put_mag(-1, jnp.where(keep, past, 0.0))
+    after = nt(x_ref[:, LEFT + raw_len - W:LEFT + raw_len + RIGHT], ft[:, 0:2 * W])
+    keep = (t < T - 1) & (lax.broadcasted_iota(jnp.int32, (rows, W), 1) < HALF_WIN)
+    put_mag(nb, jnp.where(keep, after, 0.0))
+    whiten(edge)
     for p in order[AHEAD[3]:]:
         all_bulk(p)
     pltpu.make_async_copy(recv3, recv3, r3_sem).wait()
@@ -475,7 +475,9 @@
     zero = jnp.zeros((SLAB, W), jnp.float32)
     before = [zero] * STEPS
     turned = [[zero] * group] * STEPS
+    line_ref[:, 0:W] = jnp.zeros((STEPS * SLAB, W), jnp.bfloat16)
     for q in range(T * nb + 1):
+        plain = []
         for step in range(STEPS):
             if q < T * nb:
                 top = (q % 2 * STEPS + step) * SLAB
@@ -483,6 +485,7 @@
                 turn = [x] + [pltpu.roll(x, k, 1) for k in range(1, group)]
             else:
                 x, turn = zero, [zero] * group
+            plain.append(x)
             for k in range(1, group):
                 x = jnp.where(
                     low == k, jnp.where(lane >= k, turn[k], turned[step][k]), x
@@ -492,6 +495,10 @@
             window_ref[at:at + SLAB, 0:W] = before[step]
             window_ref[at:at + SLAB, W:] = x
             before[step] = x
+        if q < T * nb - 1:
+            line_ref[:, (q + 1) * W:(q + 2) * W] = jnp.concatenate(plain, axis=0).astype(
+                jnp.bfloat16
+            )
     batch = 12
     for q in range(0, T * nb + 1, batch):
         count = min(batch, T * nb + 1 - q)
@@ -515,7 +522,7 @@
 
     def products(starts, count, fresh=False):
         w = jnp.concatenate([white_ref[:, pl.ds(aligned(n), count)] for n in starts], axis=1)
-        for k in range(0, groups, 2):
+        for k in range(0, groups - 1, 2):
             b = jnp.concatenate(
                 [
                     jnp.concatenate(
@@ -523,7 +530,7 @@
                             shifted[
                                 pl.ds(pl.multiple_of(n + 2 * HALF_LAG - lags * m, 16), count), :
                             ]
-                            for m in range(k, min(k + 2, groups))
+                            for m in range(k, k + 2)
                         ],
                         axis=1,
                     )
@@ -537,6 +544,11 @@
                 acc_ref[:, cols] = out
             else:
                 acc_ref[:, cols] += out
+        behind = jnp.concatenate([line_ref[:, pl.ds(aligned(n), count)] for n in starts], axis=1)
+        if fresh:
+            far_ref[...] = nt(behind, w)
+        else:
+            far_ref[...] += nt(behind, w)
 
     for q in range(0, dec_len, min(BLOCK, dec_len)):
         products([mine + q], min(BLOCK, dec_len), q == 0)
@@ -560,12 +572,14 @@
     else:
         lax.fori_loop(1, T, arrivals, 0)
 
-    for k in range(groups):
+    for k in range(groups - 1):
         block = acc_ref[:, k * W:(k + 1) * W].T * scale
         for step in range(STEPS):
             to = (step * LAGS + k * lags) * step_len
-            size = tall if k < groups - 1 else step_len
-            out_ref[to:to + size, :] = block[step * tall:step * tall + size, :]
+            out_ref[to:to + tall, :] = block[step * tall:(step + 1) * tall, :]
+    for step in range(STEPS):
+        to = (step * LAGS + 2 * HALF_LAG) * step_len
+        out_ref[to:to + step_len, :] = far_ref[step * SLAB:step * SLAB + step_len, :] * scale
 
     @pl.when(t < T - 1)
     def _():
@@ -626,7 +640,9 @@
             pltpu.VMEM(((T * nb + 1) * STEPS * SLAB, 2 * W), f32),
             pltpu.VMEM((2 * W, W // ns * step_len // SLAB * W), bf),
             pltpu.VMEM((total + 2 * W, W), bf),
-            pltpu.VMEM((rows, groups * W), f32),
+            pltpu.VMEM((rows, groups * W - W), f32),
+            pltpu.VMEM((STEPS * SLAB, total), bf),
+            pltpu.VMEM((STEPS * SLAB, rows), f32),
             pltpu.SemaphoreType.DMA((2,)),
             pltpu.SemaphoreType.DMA((half,)),
             pltpu.SemaphoreType.DMA((2,)),

time: 23.4 us -> 23.2 us (level)
  no operation moved by 1% of the time
where the time goes in v6:
time: 23.2 us; the launch traced here: 23.1 us
  Pallas kernels  22.1 us (95%)
  local copies, waits for them, and re-layouts  0.97 us (4%)
    pallas_call x1, Pallas kernels, per_device(): pl.pallas_call(functools.partial(kernel, C, T, 1.0 / math.sqrt(total)), o...  22.1 us
    unnamed x1, local copies, waits for them, and re-layouts  0.97 us

profile of v6, /device:TPU:0, one launch (start us, length us, event | category | flops | bytes accessed | tf_op | source)
XLA Modules:
  0.0 23.1 jit_solution(2830828015089129993)
XLA Ops:
  0.0 22.1 %shard_map.37 = f32[2056,128]{1,0:T(8,128)S(1)} custom-call(bf16[128,8192]{1,0:T(8,128)(2,1)} %raw_ref.1, bf16[1,64]{1,0:T(2,128)(2,1)} %bitcast.5, s32[2,8]{1,0:T(2,128)} %src_hbm.1), custom_call_target="tpu_custom_call" | custom-call | tf_op jit(solution)/shard_map/pallas_call | solution.py:614
  22.1 1.0 %copy.5 = f32[2,4,257,128]{3,1,2,0:T(4,128)} copy(f32[2,4,257,128]{3,1,2,0:T(4,128)S(1)} %bitcast.4) | data formatting | bytes 2105344

commit v7 on v6

--- a/solution.py
+++ b/solution.py
@@ -80,15 +80,15 @@
         pl.semaphore_signal(barrier, inc=1, device_id=along(d), device_id_type=MESH)
         return 0
 
-    lax.fori_loop(1, Z, greet_along, 0)
-    lax.fori_loop(1, near, greet_beside, 0)
-
     small = [
         pltpu.make_async_copy(taps_hbm, taps_ref, small_sem.at[0]),
         pltpu.make_async_copy(src_hbm, src_ref, small_sem.at[1]),
     ]
     for copy in small:
         copy.start()
+    lax.fori_loop(1, Z, greet_along, 0)
+    lax.fori_loop(1, near, greet_beside, 0)
+
     seg = raw_len // half
     loads = []
     for i in range(half):
@@ -282,7 +282,7 @@
 
     def outer(kind, e, g):
         to_l = e * (LOCAL - 1)
-        slot = jnp.where(kind == 0, t, t - 1)
+        slot = jnp.minimum(t, T - 2) if kind == 0 else jnp.maximum(t - 1, 0)
         inside = t < T - 1 if kind == 0 else t > 0
         same = (to_l == l) & (g == t)
         copy = pltpu.make_async_remote_copy(

time: 23.2 us -> 23 us (level)
  Pallas kernels: 22.1 us -> 21.8 us
where the time goes in v7:
time: 23 us; the launch traced here: 22.8 us
  Pallas kernels  21.8 us (95%)
  local copies, waits for them, and re-layouts  0.97 us (4%)
    pallas_call x1, Pallas kernels, per_device(): pl.pallas_call(functools.partial(kernel, C, T, 1.0 / math.sqrt(total)), o...  21.8 us
    unnamed x1, local copies, waits for them, and re-layouts  0.97 us

profile of v7, /device:TPU:0, one launch (start us, length us, event | category | flops | bytes accessed | tf_op | source)
XLA Modules:
  0.0 22.8 jit_solution(16526669130900493410)
XLA Ops:
  0.0 21.8 %shard_map.37 = f32[2056,128]{1,0:T(8,128)S(1)} custom-call(bf16[128,8192]{1,0:T(8,128)(2,1)} %raw_ref.1, bf16[1,64]{1,0:T(2,128)(2,1)} %bitcast.5, s32[2,8]{1,0:T(2,128)} %src_hbm.1), custom_call_target="tpu_custom_call" | custom-call | tf_op jit(solution)/shard_map/pallas_call | solution.py:614
  21.9 1.0 %copy.5 = f32[2,4,257,128]{3,1,2,0:T(4,128)} copy(f32[2,4,257,128]{3,1,2,0:T(4,128)S(1)} %bitcast.4) | data formatting | bytes 2105344
